TPU v7x, 128 devices: a whole 4x4x4 slice. The times are simulated.
128 devices in a mesh: lat: 8 (over x_lo, z), lon: 16 (over y, x_hi, core).
Axes of the slice: x: 4 (x_hi: 2, x_lo: 2; x = x_hi * 2 + x_lo), y: 4, z: 4, core: 2. Of those that a mesh axis runs over, the one named last changes fastest.
Arguments:
- features: bfloat16 [65536, 64], P(('lat', 'lon')), may hold values from -6 to 6
- land_tile: int32 [65536, 1], P(('lat', 'lon')), may hold values from 0 to 127; in each aligned block of 512 rows (0 to 511, 512 to 1023, ...) at most 8 rows name the same one
- land_spot: int32 [65536], P(('lat', 'lon')), may hold values from 0 to 1023
- w_in: bfloat16 [64, 256], replicated, may hold values from -0.75 to 0.75
- b_in: float32 [256], replicated, may hold values from -3 to 3
- w_mid: bfloat16 [256, 256], replicated, may hold values from -0.375 to 0.375
- b_mid: float32 [256], replicated, may hold values from -3 to 3
- w_out: bfloat16 [256, 16], replicated, may hold values from -0.375 to 0.375
- tracers: float32 [16, 16, 64, 2048], P(None, None, 'lat', 'lon'), may hold values from -6 to 6
- zonal_wind: float32 [16, 64, 2048], P(None, 'lat', 'lon'), may hold values from -0.95 to 0.95
- meridional_wind: float32 [16, 64, 2048], P(None, 'lat', 'lon'), may hold values from -0.95 to 0.95
- mixing: float32 [64, 16, 16], P('lat'), may hold values from 0 to 0.8, as said below
Outputs:
- tracers_out: float32 [16, 16, 64, 2048], P(None, None, 'lat', 'lon')
Inputs may be any that keep to these rules, and one draw needn't show every extreme that they name: `land_tile`: in each aligned block of 512 rows (the land cells of one device), no tile is named by more than 8 rows, a bound that some block reaches; every tile is named somewhere. `mixing`: entries are nonnegative.
All inputs are finite; a program needn't handle non-finite values.
Results may differ from a plain program's by a relative error of at most 0.00044.
Values sent between devices are 32-bit elements; how exact they have to be, the bound alone decides.
No kernel may reach another device: no remote copies, remote signals or barrier semaphores. Data moves between devices by JAX's collectives and lax.ppermute only.
A program may use at most 64 MiB of HBM per device.

v0:
```python
import jax
import jax.numpy as jnp
from jax import lax
from jax.sharding import PartitionSpec as P

SUBSTEPS = 2


def with_halo(block, sides, width, periodic):
    for axis, dim in sides:
        count = lax.axis_size(axis)
        forward = [(i, i + 1) for i in range(count - 1)]
        if periodic:
            forward.append((count - 1, 0))
        backward = [(target, source) for source, target in forward]
        low = lax.ppermute(
            lax.slice_in_dim(block, block.shape[dim] - width, None, axis=dim), axis, forward
        )
        high = lax.ppermute(lax.slice_in_dim(block, 0, width, axis=dim), axis, backward)
        block = jnp.concatenate([low, block, high], axis=dim)
    return block


def section(values, start, stop, axis):
    return lax.slice_in_dim(values, start, values.shape[axis] + stop, axis=axis)


def transport(values, courant, axis):
    edges = 7.0 / 12.0 * (
        section(values, 1, -2, axis) + section(values, 2, -1, axis)
    ) - 1.0 / 12.0 * (section(values, 0, -3, axis) + section(values, 3, 0, axis))
    left_edge = section(edges, 0, -1, axis)
    right_edge = section(edges, 1, 0, axis)
    centre = section(values, 2, -2, axis)
    slope = right_edge - left_edge
    curve = 6.0 * (centre - 0.5 * (left_edge + right_edge))
    face_courant = section(courant, 2, -3, axis)
    upwind = face_courant * (
        section(right_edge, 0, -1, axis)
        - 0.5
        * face_courant
        * (
            section(slope, 0, -1, axis)
            - (1.0 - 2.0 / 3.0 * face_courant) * section(curve, 0, -1, axis)
        )
    )
    reverse = -face_courant
    backward = face_courant * (
        section(left_edge, 1, 0, axis)
        + 0.5
        * reverse
        * (section(slope, 1, 0, axis) + (1.0 - 2.0 / 3.0 * reverse) * section(curve, 1, 0, axis))
    )
    crossing = jnp.where(face_courant >= 0, upwind, backward)
    return section(values, 3, -3, axis) - (
        section(crossing, 1, 0, axis) - section(crossing, 0, -1, axis)
    )


def on_device(
    features,
    land_tile,
    land_spot,
    w_in,
    b_in,
    w_mid,
    b_mid,
    w_out,
    tracers,
    zonal_wind,
    meridional_wind,
    mixing,
):
    first = jax.nn.silu(jnp.dot(features, w_in, preferred_element_type=jnp.float32) + b_in).astype(
        jnp.bfloat16
    )
    second = jax.nn.silu(jnp.dot(first, w_mid, preferred_element_type=jnp.float32) + b_mid).astype(
        jnp.bfloat16
    )
    surface_flux = jnp.dot(second, w_out, preferred_element_type=jnp.float32)
    tracer_count = surface_flux.shape[1]
    lat_count = lax.axis_size("lat")
    lon_count = lax.axis_size("lon")
    device_count = lat_count * lon_count
    capacity = 2 * surface_flux.shape[0] // device_count
    owner_tile = land_tile[:, 0]
    member = (owner_tile[:, None] == jnp.arange(device_count, dtype=jnp.int32)[None, :]).astype(
        jnp.int32
    )
    earlier = jnp.cumsum(member, axis=0) - member
    slot_index = jnp.sum(earlier * member, axis=1)
    outgoing = (
        jnp.zeros((device_count, capacity, tracer_count), jnp.float32)
        .at[owner_tile, slot_index]
        .set(surface_flux)
    )
    places = (
        jnp.zeros((device_count, capacity), jnp.float32)
        .at[owner_tile, slot_index]
        .set(land_spot.astype(jnp.float32))
    )
    arrived_flux, arrived_places = (
        lax.all_to_all(outgoing, ("lat", "lon"), split_axis=0, concat_axis=0, tiled=True),
        lax.all_to_all(places, ("lat", "lon"), split_axis=0, concat_axis=0, tiled=True),
    )
    _, levels, tile_rows, tile_cols = tracers.shape
    positions = arrived_places.reshape(-1).astype(jnp.int32)
    emitted = (
        jnp.zeros((tile_rows * tile_cols, tracer_count), jnp.float32)
        .at[positions]
        .add(arrived_flux.reshape(-1, tracer_count))
    )
    state = tracers.at[:, 0].add(emitted.T.reshape(tracer_count, tile_rows, tile_cols))
    global_rows = lax.axis_index("lat") * tile_rows + jnp.arange(tile_rows, dtype=jnp.int32)
    northern = (global_rows < tile_rows * lat_count - 1).astype(jnp.float32)
    meridional = (meridional_wind * northern[None, :, None])[None]
    zonal = zonal_wind[None]
    for substep in range(SUBSTEPS):
        joined = jnp.concatenate([state, zonal], axis=0)
        widened = with_halo(joined, (("lon", 3),), 3, True)
        state = transport(widened[:-1], widened[-1:], 3)
    for substep in range(SUBSTEPS):
        joined = jnp.concatenate([state, meridional], axis=0)
        widened = with_halo(joined, (("lat", 2),), 3, False)
        state = transport(widened[:-1], widened[-1:], 2)
    return jnp.einsum("akj,tjab->tkab", mixing, state, precision=lax.Precision.HIGHEST)


def solution(mesh):
    placed = (
        P(("lat", "lon"), None),
        P(("lat", "lon"), None),
        P(("lat", "lon")),
        P(),
        P(),
        P(),
        P(),
        P(),
        P(None, None, "lat", "lon"),
        P(None, "lat", "lon"),
        P(None, "lat", "lon"),
        P("lat", None, None),
    )
    return jax.shard_map(
        on_device,
        mesh=mesh,
        in_specs=placed,
        out_specs=P(None, None, "lat", "lon"),
        check_vma=False,
    )
```

profile of v0, /device:TPU:2, one launch (start us, length us, event | category | flops | bytes accessed | tf_op | source)
XLA Modules:
  0.0 170.8 jit_solution(7623290489217367102)
XLA Ops:
  0.0 0.7 convert_element_type.38
  0.7 0.8 copy.101
  1.8 0.9 fusion.83
  2.7 0.7 or_select_fusion
  3.5 22.0 %scatter_fusion = f32[128,8]{0,1:T(8,128)S(1)} fusion(f32[128,8]{0,1:T(8,128)S(1)} %broadcast_in_dim.59, s32[512]{0:T(512)S(1)} %bitcast.92, f32[512]{0:T(512)S(1)} %convert_element_type.38), kind=kCustom, calls=%fused_computation | custom fusion | bytes 10240 | tf_op jit(solution)/shard_map/scatter | solution.py:100
  25.5 0.7 copy.103
  26.2 10.5 %all-to-all-start = ((f32[128,1,8]{2,1,0:T(1,128)}), f32[128,1,8]{2,1,0:T(1,128)S(1)}, u32[]{:S(2)}, u32[]{:S(2)}) async-start(f32[128,1,8]{2,1,0:T(1,128)} %copy.103), calls=%async_computation | async-start | bytes 131072 | tf_op jit(solution)/shard_map/all_to_all | solution.py:104
  36.8 0.3 multiply_convert_fusion.1
  37.2 0.4 fusion.79
  37.6 0.8 copy-done.6
  38.7 22.7 %scatter_fusion.1 = f32[128,8,16]{2,1,0:T(8,128)S(1)} fusion(f32[128,8,16]{2,1,0:T(8,128)S(1)} %broadcast_in_dim.60, s32[512]{0:T(512)S(1)} %bitcast.93, f32[512,16]{1,0:T(8,128)S(1)} %fusion.79), kind=kCustom, calls=%fused_computation.1 | custom fusion | bytes 102400 | tf_op jit(solution)/shard_map/scatter | solution.py:95
  61.4 0.9 reshape.136
  62.3 9.8 %all-to-all-start.1 = ((f32[128,1,128]{2,1,0:T(1,128)}), f32[128,1,128]{2,1,0:T(1,128)S(1)}, u32[]{:S(2)}, u32[]{:S(2)}) async-start(f32[128,1,128]{2,1,0:T(1,128)} %reshape.136), calls=%async_computation.1 | async-start | bytes 131072 | tf_op jit(solution)/shard_map/all_to_all | solution.py:103
  72.4 8.5 %all-to-all-done.1 = f32[128,1,128]{2,1,0:T(1,128)S(1)} async-done(((f32[128,1,128]{2,1,0:T(1,128)}), f32[128,1,128]{2,1,0:T(1,128)S(1)}, u32[]{:S(2)}, u32[]{:S(2)}) %all-to-all-start.1) | async-done | bytes 65568 | tf_op jit(solution)/shard_map/all_to_all | solution.py:103
  80.9 0.5 broadcast.257
  81.4 0.8 reduce.6
  82.4 6.2 %scatter_custom_fusion.2 = f32[1024,16]{1,0:T(8,128)S(1)} fusion(s32[1024]{0:T(1024)S(1)} %bitcast.103, f32[128,8,16]{2,1,0:T(8,128)S(1)} %reshape.137, f32[]{:T(128)} %constant.64.clone.1), kind=kCustom, calls=%fused_computation.129 | custom fusion | flops 16384 | bytes 589828 | tf_op jit(solution)/shard_map/scatter-add | solution.py:111
  88.8 1.3 scatter-add.13
  90.2 0.4 slice_maximum_fusion.1
  90.5 1.7 copy.109
  92.2 1.0 copy.115
  93.2 5.6 %collective-permute-start.1 = (f32[17,16,8,3]{0,2,3,1:T(8,128)S(1)}, f32[17,16,8,3]{0,2,3,1:T(8,128)}, u32[]{:S(2)}, u32[]{:S(2)}) collective-permute-start(f32[17,16,8,3]{0,2,3,1:T(8,128)S(1)} %copy.115), channel_id=1, source_target_pairs={{1,0},{2,1},{3,2},{4,3},{5,4},{6,5},{7,6},{8,7},{9,8},{10,9},{11,1... | collective-permute-start | bytes 78344 | tf_op jit(solution)/shard_map/ppermute | solution.py:19
  98.8 3.1 %collective-permute-done = f32[17,16,8,3]{0,2,3,1:T(8,128)S(1)} collective-permute-done((f32[17,16,8,3]{0,2,3,1:T(8,128)}, f32[17,16,8,3]{0,2,3,1:T(8,128)S(1)}, u32[]{:S(2)}, u32[]{:S(2)}) %collective-permute-start) | collective-permute-done | bytes 26144 | tf_op jit(solution)/shard_map/ppermute | solution.py:16
  101.9 1.2 copy.110
  103.1 0.7 fusion.4
  103.8 1.1 slice_bitcast_fusion.1
  105.0 0.3 copy-done.4
  105.3 2.1 %copy.117 = f32[17,16,8,3]{3,1,2,0:T(8,128)S(1)} copy(f32[17,16,8,3]{0,2,3,1:T(8,128)} %collective-permute-done.1) | data formatting | bytes 52224 | tf_op jit(solution)/shard_map/ppermute | solution.py:19
  107.5 0.9 fusion.1
  108.4 0.7 copy-done.5
  109.1 1.2 fusion.9
  110.4 1.2 slice_subtract_fusion.3
  111.6 1.7 fusion.29
  113.3 0.4 fusion.75
  113.7 0.4 slice_maximum_fusion
  114.1 1.7 copy.128
  115.9 1.0 copy.134
  116.8 5.6 %collective-permute-start.3 = (f32[17,16,8,3]{0,2,3,1:T(8,128)S(1)}, f32[17,16,8,3]{0,2,3,1:T(8,128)}, u32[]{:S(2)}, u32[]{:S(2)}) collective-permute-start(f32[17,16,8,3]{0,2,3,1:T(8,128)S(1)} %copy.134), channel_id=1, source_target_pairs={{1,0},{2,1},{3,2},{4,3},{5,4},{6,5},{7,6},{8,7},{9,8},{10,9},{11,1... | collective-permute-start | bytes 78344 | tf_op jit(solution)/shard_map/ppermute | solution.py:19
  122.5 3.1 %collective-permute-done.2 = f32[17,16,8,3]{0,2,3,1:T(8,128)S(1)} collective-permute-done((f32[17,16,8,3]{0,2,3,1:T(8,128)}, f32[17,16,8,3]{0,2,3,1:T(8,128)S(1)}, u32[]{:S(2)}, u32[]{:S(2)}) %collective-permute-start.2) | collective-permute-done | bytes 26144 | tf_op jit(solution)/shard_map/ppermute | solution.py:16
  125.6 1.2 copy.129
  126.8 0.7 fusion.5
  127.5 1.1 slice_bitcast_fusion
  128.7 0.3 copy-done.2
  129.1 2.1 %copy.136 = f32[17,16,8,3]{3,1,2,0:T(8,128)S(1)} copy(f32[17,16,8,3]{0,2,3,1:T(8,128)} %collective-permute-done.3) | data formatting | bytes 52224 | tf_op jit(solution)/shard_map/ppermute | solution.py:19
  131.2 0.9 fusion.3
  132.2 0.7 copy-done.3
  132.9 1.2 fusion.13
  134.1 1.2 slice_subtract_fusion.2
  135.4 1.7 fusion.18
  137.1 0.4 fusion.74
  137.5 2.6 %collective-permute-start.4 = (f32[17,16,3,128]{3,1,2,0:T(8,128)S(1)}, f32[17,16,3,128]{3,1,2,0:T(8,128)S(1)}, u32[]{:S(2)}, u32[]{:S(2)}) collective-permute-start(f32[17,16,3,128]{3,1,2,0:T(8,128)S(1)} %get-tuple-element.47), channel_id=1, source_target_pairs={{0,16},{16,32},{32,48},{48,64},{64,80},{80,96},{96,112},{1,17},{17... | collective-permute-start | bytes 1253384 | tf_op jit(solution)/shard_map/ppermute | solution.py:16
  140.1 5.4 %collective-permute-start.5 = (f32[17,16,3,128]{3,1,2,0:T(8,128)S(1)}, f32[17,16,3,128]{3,1,2,0:T(8,128)S(1)}, u32[]{:S(2)}, u32[]{:S(2)}) collective-permute-start(f32[17,16,3,128]{3,1,2,0:T(8,128)S(1)} %get-tuple-element.48), channel_id=1, source_target_pairs={{16,0},{32,16},{48,32},{64,48},{80,64},{96,80},{112,96},{17,1},{33... | collective-permute-start | bytes 1253384 | tf_op jit(solution)/shard_map/ppermute | solution.py:19
  145.5 4.1 %collective-permute-done.4 = f32[17,16,3,128]{3,1,2,0:T(8,128)S(1)} collective-permute-done((f32[17,16,3,128]{3,1,2,0:T(8,128)S(1)}, f32[17,16,3,128]{3,1,2,0:T(8,128)S(1)}, u32[]{:S(2)}, u32[]{:S(2)}) %collective-permute-start.4) | collective-permute-done | bytes 417824 | tf_op jit(solution)/shard_map/ppermute | solution.py:16
  149.8 1.3 collective-permute-done.5
  151.9 0.4 fusion.67
  152.6 1.9 %collective-permute-start.6 = (f32[17,16,3,128]{3,1,2,0:T(8,128)S(1)}, f32[17,16,3,128]{3,1,2,0:T(8,128)S(1)}, u32[]{:S(2)}, u32[]{:S(2)}) collective-permute-start(f32[17,16,3,128]{3,1,2,0:T(8,128)S(1)} %get-tuple-element.45), channel_id=1, source_target_pairs={{0,16},{16,32},{32,48},{48,64},{64,80},{80,96},{96,112},{1,17},{17... | collective-permute-start | bytes 1253384 | tf_op jit(solution)/shard_map/ppermute | solution.py:16
  154.5 6.8 %collective-permute-start.7 = (f32[17,16,3,128]{3,1,2,0:T(8,128)S(1)}, f32[17,16,3,128]{3,1,2,0:T(8,128)S(1)}, u32[]{:S(2)}, u32[]{:S(2)}) collective-permute-start(f32[17,16,3,128]{3,1,2,0:T(8,128)S(1)} %get-tuple-element.46), channel_id=1, source_target_pairs={{16,0},{32,16},{48,32},{64,48},{80,64},{96,80},{112,96},{17,1},{33... | collective-permute-start | bytes 1253384 | tf_op jit(solution)/shard_map/ppermute | solution.py:19
  161.3 3.8 %collective-permute-done.6 = f32[17,16,3,128]{3,1,2,0:T(8,128)S(1)} collective-permute-done((f32[17,16,3,128]{3,1,2,0:T(8,128)S(1)}, f32[17,16,3,128]{3,1,2,0:T(8,128)S(1)}, u32[]{:S(2)}, u32[]{:S(2)}) %collective-permute-start.6) | collective-permute-done | bytes 417824 | tf_op jit(solution)/shard_map/ppermute | solution.py:16
  165.3 1.3 collective-permute-done.7
  166.7 0.3 fusion.49
  167.3 0.4 fusion.58
  167.8 0.4 copy-done.16
  168.1 1.1 convolution_bitcast_fusion
  169.2 1.6 copy.149
  (85 shorter events, 3.6 us)
Async XLA Ops:
  0.0 37.1 %copy-start = (bf16[256,256]{1,0:T(8,128)(2,1)S(1)}, bf16[256,256]{1,0:T(8,128)(2,1)}, u32[]{:S(2)}) copy-start(bf16[256,256]{1,0:T(8,128)(2,1)} %param.19) | copy-start | bytes 393220
  3.5 33.3 %copy-start.19 = (bf16[512,64]{0,1:T(8,128)(2,1)S(1)}, bf16[512,64]{0,1:T(8,128)(2,1)}, u32[]{:S(2)}) copy-start(bf16[512,64]{0,1:T(8,128)(2,1)} %param.14) | copy-start | bytes 196612
  3.5 33.3 %copy-start.20 = (bf16[64,256]{1,0:T(8,128)(2,1)S(1)}, bf16[64,256]{1,0:T(8,128)(2,1)}, u32[]{:S(2)}) copy-start(bf16[64,256]{1,0:T(8,128)(2,1)} %param.17) | copy-start | bytes 98308
  3.5 33.3 %copy-start.22 = (f32[256]{0:T(256)S(1)}, f32[256]{0:T(256)}, u32[]{:S(2)}) copy-start(f32[256]{0:T(256)} %param.18) | copy-start | bytes 3076
  25.5 11.7 %copy-start.21 = (bf16[256,16]{0,1:T(8,128)(2,1)S(1)}, bf16[256,16]{0,1:T(8,128)(2,1)}, u32[]{:S(2)}) copy-start(bf16[256,16]{0,1:T(8,128)(2,1)} %param.21) | copy-start | bytes 24580
  25.5 11.7 %copy-start.23 = (f32[256]{0:T(256)S(1)}, f32[256]{0:T(256)}, u32[]{:S(2)}) copy-start(f32[256]{0:T(256)} %param.20) | copy-start | bytes 3076
  26.2 36.0 %all-to-all-start = ((f32[128,1,8]{2,1,0:T(1,128)}), f32[128,1,8]{2,1,0:T(1,128)S(1)}, u32[]{:S(2)}, u32[]{:S(2)}) async-start(f32[128,1,8]{2,1,0:T(1,128)} %copy.103), calls=%async_computation | async-start | bytes 131072 | tf_op jit(solution)/shard_map/all_to_all | solution.py:104
  37.2 1.2 copy-start.6
  37.2 1.4 copy-start.17
  61.4 27.3 %slice-start = ((f32[16,16,8,128]{3,2,1,0:T(8,128)}), f32[16,1,8,128]{3,2,1,0:T(8,128)S(1)}, s32[]{:S(2)}) async-start(f32[16,16,8,128]{3,2,1,0:T(8,128)} %param.22), calls=%async_computation.2 | async-start | bytes 131072 | tf_op jit(solution)/shard_map/slice.78
  62.3 18.6 %all-to-all-start.1 = ((f32[128,1,128]{2,1,0:T(1,128)}), f32[128,1,128]{2,1,0:T(1,128)S(1)}, u32[]{:S(2)}, u32[]{:S(2)}) async-start(f32[128,1,128]{2,1,0:T(1,128)} %reshape.136), calls=%async_computation.1 | async-start | bytes 131072 | tf_op jit(solution)/shard_map/all_to_all | solution.py:103
  92.2 9.7 %collective-permute-start = (f32[17,16,8,3]{0,2,3,1:T(8,128)}, f32[17,16,8,3]{0,2,3,1:T(8,128)S(1)}, u32[]{:S(2)}, u32[]{:S(2)}) collective-permute-start(f32[17,16,8,3]{0,2,3,1:T(8,128)} %copy.109), channel_id=1, source_target_pairs={{0,1},{1,2},{2,3},{3,4},{4,5},{5,6},{6,7},{7,8},{8,9},{9,10},{10,1... | collective-permute-start | bytes 78344 | tf_op jit(solution)/shard_map/ppermute | solution.py:16
  93.2 12.1 %collective-permute-start.1 = (f32[17,16,8,3]{0,2,3,1:T(8,128)S(1)}, f32[17,16,8,3]{0,2,3,1:T(8,128)}, u32[]{:S(2)}, u32[]{:S(2)}) collective-permute-start(f32[17,16,8,3]{0,2,3,1:T(8,128)S(1)} %copy.115), channel_id=1, source_target_pairs={{1,0},{2,1},{3,2},{4,3},{5,4},{6,5},{7,6},{8,7},{9,8},{10,9},{11,1... | collective-permute-start | bytes 78344 | tf_op jit(solution)/shard_map/ppermute | solution.py:19
  103.8 1.5 copy-start.4
  107.5 1.6 copy-start.5
  110.3 1.2 copy-start.12
  110.3 1.2 copy-start.13
  110.3 1.2 copy-start.14
  110.4 1.2 copy-start.15
  113.7 2.1 %copy-start.18 = (f32[16,8,128]{2,1,0:T(8,128)S(1)}, f32[16,8,128]{2,1,0:T(8,128)}, u32[]{:S(2)}) copy-start(f32[16,8,128]{2,1,0:T(8,128)} %param.24) | copy-start | bytes 196612
  115.8 9.8 %collective-permute-start.2 = (f32[17,16,8,3]{0,2,3,1:T(8,128)}, f32[17,16,8,3]{0,2,3,1:T(8,128)S(1)}, u32[]{:S(2)}, u32[]{:S(2)}) collective-permute-start(f32[17,16,8,3]{0,2,3,1:T(8,128)} %copy.128), channel_id=1, source_target_pairs={{0,1},{1,2},{2,3},{3,4},{4,5},{5,6},{6,7},{7,8},{8,9},{9,10},{10,1... | collective-permute-start | bytes 78344 | tf_op jit(solution)/shard_map/ppermute | solution.py:16
  116.8 12.2 %collective-permute-start.3 = (f32[17,16,8,3]{0,2,3,1:T(8,128)S(1)}, f32[17,16,8,3]{0,2,3,1:T(8,128)}, u32[]{:S(2)}, u32[]{:S(2)}) collective-permute-start(f32[17,16,8,3]{0,2,3,1:T(8,128)S(1)} %copy.134), channel_id=1, source_target_pairs={{1,0},{2,1},{3,2},{4,3},{5,4},{6,5},{7,6},{8,7},{9,8},{10,9},{11,1... | collective-permute-start | bytes 78344 | tf_op jit(solution)/shard_map/ppermute | solution.py:19
  127.5 1.6 copy-start.2
  131.2 1.6 copy-start.3
  134.1 1.2 copy-start.7
  134.1 1.2 copy-start.8
  134.1 1.2 copy-start.9
  134.1 1.2 copy-start.10
  134.1 1.2 copy-start.11
  137.5 12.0 %collective-permute-start.4 = (f32[17,16,3,128]{3,1,2,0:T(8,128)S(1)}, f32[17,16,3,128]{3,1,2,0:T(8,128)S(1)}, u32[]{:S(2)}, u32[]{:S(2)}) collective-permute-start(f32[17,16,3,128]{3,1,2,0:T(8,128)S(1)} %get-tuple-element.47), channel_id=1, source_target_pairs={{0,16},{16,32},{32,48},{48,64},{64,80},{80,96},{96,112},{1,17},{17... | collective-permute-start | bytes 1253384 | tf_op jit(solution)/shard_map/ppermute | solution.py:16
  140.1 10.9 %collective-permute-start.5 = (f32[17,16,3,128]{3,1,2,0:T(8,128)S(1)}, f32[17,16,3,128]{3,1,2,0:T(8,128)S(1)}, u32[]{:S(2)}, u32[]{:S(2)}) collective-permute-start(f32[17,16,3,128]{3,1,2,0:T(8,128)S(1)} %get-tuple-element.48), channel_id=1, source_target_pairs={{16,0},{32,16},{48,32},{64,48},{80,64},{96,80},{112,96},{17,1},{33... | collective-permute-start | bytes 1253384 | tf_op jit(solution)/shard_map/ppermute | solution.py:19
  152.6 12.5 %collective-permute-start.6 = (f32[17,16,3,128]{3,1,2,0:T(8,128)S(1)}, f32[17,16,3,128]{3,1,2,0:T(8,128)S(1)}, u32[]{:S(2)}, u32[]{:S(2)}) collective-permute-start(f32[17,16,3,128]{3,1,2,0:T(8,128)S(1)} %get-tuple-element.45), channel_id=1, source_target_pairs={{0,16},{16,32},{32,48},{48,64},{64,80},{80,96},{96,112},{1,17},{17... | collective-permute-start | bytes 1253384 | tf_op jit(solution)/shard_map/ppermute | solution.py:16
  154.5 12.0 %collective-permute-start.7 = (f32[17,16,3,128]{3,1,2,0:T(8,128)S(1)}, f32[17,16,3,128]{3,1,2,0:T(8,128)S(1)}, u32[]{:S(2)}, u32[]{:S(2)}) collective-permute-start(f32[17,16,3,128]{3,1,2,0:T(8,128)S(1)} %get-tuple-element.46), channel_id=1, source_target_pairs={{16,0},{32,16},{48,32},{64,48},{80,64},{96,80},{112,96},{17,1},{33... | collective-permute-start | bytes 1253384 | tf_op jit(solution)/shard_map/ppermute | solution.py:19
  167.3 0.8 copy-start.16
  167.3 3.5 %copy-start.1 = (bf16[256,256]{1,0:T(8,128)(2,1)S(1)}, bf16[256,256]{1,0:T(8,128)(2,1)}, u32[]{:S(2)}) copy-start(bf16[256,256]{1,0:T(8,128)(2,1)} %param.19) | copy-start | bytes 393220
where the time goes:
time: 173 us; the launch traced here: 171 us
  local copies, waits for them, and re-layouts  66.6 us (38%)
  starting transfers between devices  48.2 us (28%)
  other arithmetic  28.3 us (16%)
  waiting for transfers between devices  25.1 us (15%)
  matrix products  1.82 us (1%)
    ppermute x4, starting transfers between devices, with_halo(): lax.ppermute(lax.slice_in_dim(block, 0, width, axis=dim), axis, backward)  23.3 us
    scatter x1, local copies, waits for them, and re-layouts, on_device(): outgoing = jnp.zeros((device_count, capacity, tracer_count), jnp.float32)...  22.7 us
    scatter x1, local copies, waits for them, and re-layouts, on_device(): places = jnp.zeros((device_count, capacity), jnp.float32).at[owner_tile,...  22 us
    ppermute x4, waiting for transfers between devices, with_halo(): lax.ppermute(lax.slice_in_dim(block, block.shape[dim] - width, None, axis...  14.1 us
    all_to_all x1, starting transfers between devices, on_device(): lax.all_to_all(places, ('lat', 'lon'), split_axis=0, concat_axis=0, tiled...  10.5 us
    all_to_all x1, starting transfers between devices, on_device(): lax.all_to_all(outgoing, ('lat', 'lon'), split_axis=0, concat_axis=0, til...  9.81 us
    all_to_all x1, waiting for transfers between devices, on_device(): lax.all_to_all(outgoing, ('lat', 'lon'), split_axis=0, concat_axis=0, til...  8.47 us
    scatter-add x1, other arithmetic, on_device(): emitted = jnp.zeros((tile_rows * tile_cols, tracer_count), jnp.float32).a...  6.19 us
  transfers between devices with their start and end apart: 10, of which 7 were waited for; matrix products, arithmetic and copies ran while one was open for 20% of the time, Pallas kernels for 0%

commit v1 on v0

v1 whole, which is shorter than its diff:
```python
import jax
import jax.numpy as jnp
from jax import lax
from jax.experimental import pallas as pl
from jax.experimental.pallas import tpu as pltpu
from jax.sharding import PartitionSpec as P

F32 = jnp.float32
BF16 = jnp.bfloat16
NT = (((1,), (1,)), ((), ()))
TN = (((0,), (0,)), ((), ()))
ROWS = 10
LATMSG = 17 * 12 + 2
VM = pltpu.VMEM
PARAMS = pltpu.CompilerParams(vmem_limit_bytes=48 * 1024 * 1024)


def vspec():
    return pl.BlockSpec(memory_space=VM)


def sspec():
    return pl.BlockSpec(memory_space=pltpu.SMEM)


def iota(shape, dim):
    return lax.broadcasted_iota(jnp.int32, shape, dim)


def face_weights(c):
    pos = c >= 0
    w = jnp.abs(c)
    al = 0.5 * w * w
    be = 3.0 * al - 2.0 * al * w
    p = w - al - be
    g = al - be
    h = 2.0 * be
    p = jnp.where(pos, p, -p)
    zero = jnp.zeros_like(c)
    gp = jnp.where(pos, g, zero)
    gm = jnp.where(pos, zero, -g)
    hp = jnp.where(pos, h, zero)
    hm = jnp.where(pos, zero, -h)
    a, b = 7.0 / 12.0, 1.0 / 12.0
    return [
        -b * gp,
        a * gp - b * p,
        a * (p + gp) - b * gm + hp,
        a * (p + gm) - b * gp + hm,
        a * gm - b * p,
        -b * gm,
    ]


def step_weights(f, f_before):
    out = []
    for m in range(-3, 4):
        v = None
        if m <= 2:
            v = f_before[m + 3]
        if m >= -2:
            v = -f[m + 2] if v is None else v - f[m + 2]
        if m == 0:
            v = v + 1.0
        out.append(v)
    return out


def shifted(q, low, high, s, axis, pos):
    n = q.shape[axis]
    if s == 0:
        return q
    if s > 0:
        return pltpu.roll(jnp.where(pos < s, high, q), n - s, axis)
    return pltpu.roll(jnp.where(pos >= n + s, low, q), -s, axis)


def double_weights(w, w_low, w_high, axis, pos):
    out = [None] * 13
    for a in range(-3, 4):
        for b in range(-3, 4):
            v = w[a + 3] * shifted(w[b + 3], w_low[b + 3], w_high[b + 3], a, axis, pos)
            out[a + b + 6] = v if out[a + b + 6] is None else out[a + b + 6] + v
    return out


def apply13(v, q, low, high, axis, pos):
    out = v[6] * q
    for s in range(1, 7):
        out = out + v[6 + s] * shifted(q, low, high, s, axis, pos)
        out = out + v[6 - s] * shifted(q, low, high, -s, axis, pos)
    return out


def lon_weights(c, c_halo, lane):
    f, fh = face_weights(c), face_weights(c_halo)
    before = [shifted(x, y, y, -1, 1, lane) for x, y in zip(f, fh)]
    halo_before = [shifted(y, x, x, -1, 1, lane) for x, y in zip(f, fh)]
    w, wh = step_weights(f, before), step_weights(fh, halo_before)
    return double_weights(w, wh, wh, 1, lane)


def lat_weights(c, low, high, sub):
    f, fl, fh = face_weights(c), face_weights(low), face_weights(high)
    before = [shifted(x, y, y, -1, 0, sub) for x, y in zip(f, fl)]
    low_before = [shifted(y, y, y, -1, 0, sub) for y in fl]
    high_before = [shifted(y, x, x, -1, 0, sub) for x, y in zip(f, fh)]
    w = step_weights(f, before)
    wl = step_weights(fl, low_before)
    wh = step_weights(fh, high_before)
    return double_weights(w, wl, wh, 0, sub)


def pack_kernel(ids, tracers, zonal, out_a, out_b):
    odd = (ids[1] & 1) == 1
    slot = iota((8, 128), 1) >> 3

    def pack(read):
        left = right = jnp.zeros((8, 128), F32)
        for k in range(16):
            q = read(k)
            r = q if k == 0 else pltpu.roll(q, 8 * k, 1)
            left = jnp.where(slot == k, r, left)
            right = jnp.where(slot == (k + 15) % 16, r, right)
        return jnp.where(odd, left, right), jnp.where(odd, right, left)

    def body(t, carry):
        a, b = pack(lambda k: tracers[t, k])
        out_a[t], out_b[t] = a, b
        return carry

    lax.fori_loop(0, 16, body, 0)
    a, b = pack(lambda k: zonal[k])
    out_a[16], out_b[16] = a, b


def flux_kernel(feat, tile, spot, w_in, b_in, w_mid, b_mid, w_out, out):
    def silu(v):
        return (v / (1.0 + jnp.exp(-v))).astype(BF16)

    first = silu(lax.dot_general(feat[...], w_in[...], TN, preferred_element_type=F32) + b_in[...])
    second = silu(jnp.dot(first, w_mid[...], preferred_element_type=F32) + b_mid[...])
    flux = lax.dot_general(w_out[...], second, NT, preferred_element_type=F32)
    cells = flux.shape[1]
    member = iota((128, cells), 0) == tile[...]
    member32 = jnp.where(member, 1.0, 0.0)
    member16 = member32.astype(BF16)
    upper = jnp.where(iota((cells, cells), 0) < iota((cells, cells), 1), 1.0, 0.0).astype(BF16)
    earlier = jnp.dot(member16, upper, preferred_element_type=F32)
    slot = jnp.sum(member32 * earlier, axis=0, keepdims=True).astype(jnp.int32)
    high = flux.astype(BF16).astype(F32)
    low = flux - high
    zero = jnp.zeros_like(flux)
    rows_high = jnp.concatenate([jnp.where(slot == s, high, zero) for s in range(8)], 0)
    rows_low = jnp.concatenate([jnp.where(slot == s, low, zero) for s in range(8)], 0)
    sent = lax.dot_general(
        member16, rows_high.astype(BF16), NT, preferred_element_type=F32
    ) + lax.dot_general(member16, rows_low.astype(BF16), NT, preferred_element_type=F32)
    here = (iota((128, cells), 0) & 7) == slot
    places = spot[...]
    coarse = jnp.where(here, (places >> 4) << 4, 0).astype(F32).astype(BF16)
    fine = jnp.where(here, places & 15, 0).astype(F32).astype(BF16)
    spots = lax.dot_general(member16, coarse, NT, preferred_element_type=F32) + lax.dot_general(
        member16, fine, NT, preferred_element_type=F32
    )
    row = iota((128, 128), 0)
    group = iota((128, 128), 1) >> 3

    def beside(x, dn):
        if dn == 0:
            return x
        if dn == 1:
            return jnp.where((row & 15) == 15, pltpu.roll(x, 15, 0), pltpu.roll(x, 127, 0))
        return jnp.where((row & 15) == 0, pltpu.roll(x, 113, 0), pltpu.roll(x, 1, 0))

    def above(x, dl):
        pad = jnp.zeros((16, 128), F32)
        if dl == 0:
            return x
        if dl == 1:
            return jnp.concatenate([x[16:], pad], 0)
        return jnp.concatenate([pad, x[:-16]], 0)

    places_out = jnp.zeros((128, 128), F32)
    for dn in (-1, 0, 1):
        x, y = beside(sent, dn), beside(spots, dn)
        for dl in (-1, 0, 1):
            b = (dl + 1) * 3 + dn + 1
            out[pl.ds(b, 128, stride=ROWS), :] = above(x, dl)
            places_out = jnp.where(group == b, above(y, dl), places_out)
    out[pl.ds(9, 128, stride=ROWS), :] = places_out


def lon_kernel(ids, tracers, zonal, merid, halo_a, halo_b, state, out_a, out_b):
    odd = (ids[1] & 1) == 1
    odd_lat = (ids[0] & 1) == 1
    lane = iota((8, 128), 1)
    slot = lane >> 3
    sub = iota((8, 128), 0)

    def halo(t, k):
        a, b = halo_a[t], halo_b[t]
        right, left = jnp.where(odd, b, a), jnp.where(odd, a, b)
        return pltpu.roll(jnp.where(slot == k, right, left), (128 - 8 * k) & 127, 1)

    def level(k, carry):
        v = lon_weights(zonal[k], halo(16, k), lane)
        for t in range(16):
            h = halo(t, k)
            state[t, k] = apply13(v, tracers[t, k], h, h, 1, lane)
        return carry

    lax.fori_loop(0, 16, level, 0)

    def emit(n, up, down):
        out_a[n] = jnp.where(odd_lat, down, up)
        out_b[n] = jnp.where(odd_lat, up, down)

    def pack(t, read):
        for g in range(4):
            q = [read(4 * g + i) for i in range(4)]
            for i in range(3):
                last = pltpu.roll(q[3], 6 - 2 * i, 0)
                emit(t * 12 + g * 3 + i, jnp.where(sub >= 2, q[i], last), jnp.where(sub < 6, q[i], last))

    def body(t, carry):
        pack(t, lambda k: state[t, k])
        return carry

    lax.fori_loop(0, 16, body, 0)
    keep = jnp.logical_or(sub < 7, ids[0] < 7)
    pack(16, lambda k: jnp.where(keep, merid[k], 0.0))
    emit(204, zonal[0], zonal[0])
    h = halo(16, 0)
    emit(205, h, h)


def lat_kernel(ids, state, zonal, merid, halo_a, halo_b, zonal_halo_a, zonal_halo_b, mixing, out, lonw, latw, column, swept):
    odd_lat = (ids[0] & 1) == 1
    odd = (ids[1] & 1) == 1
    lane = iota((8, 128), 1)
    sub = iota((8, 128), 0)
    keep = jnp.logical_or(sub < 7, ids[0] < 7)

    def message(n):
        a, b = halo_a[n], halo_b[n]
        return jnp.where(odd_lat, a, b), jnp.where(odd_lat, b, a)

    def four(t, g):
        got = [message(t * 12 + g * 3 + i) for i in range(3)]
        pairs = list(got)
        rolled = [[pltpu.roll(got[i][j], 2 + 2 * i, 0) for i in range(3)] for j in range(2)]
        low = jnp.where(sub < 4, rolled[0][0], jnp.where(sub < 6, rolled[0][1], rolled[0][2]))
        high = jnp.where(sub < 2, rolled[1][0], jnp.where(sub < 4, rolled[1][1], rolled[1][2]))
        pairs.append((low, high))
        return pairs

    def group(g, carry):
        winds = four(16, g)
        weights = [
            lat_weights(jnp.where(keep, merid[4 * g + i], 0.0), winds[i][0], winds[i][1], sub)
            for i in range(4)
        ]

        for i in range(4):
            for m in range(13):
                latw[4 * g + i, m] = weights[i][m]

        def tracer(t, c):
            halos = four(t, g)
            for i in range(4):
                v = [latw[4 * g + i, m] for m in range(13)]
                swept[t, pl.ds(32 * g + 8 * i, 8), :] = apply13(
                    v, state[t, 4 * g + i], halos[i][0], halos[i][1], 0, sub
                )
            return c

        return lax.fori_loop(0, 16, tracer, carry)

    lax.fori_loop(0, 4, group, 0)
    slot = lane >> 3
    a, b = zonal_halo_a[16], zonal_halo_b[16]
    own = jnp.where(slot == 0, jnp.where(odd, b, a), jnp.where(odd, a, b))
    wind, wind_halo = message(204), message(205)
    for n, (c, h) in enumerate(((wind[0], wind_halo[0]), (zonal[0], own), (wind[1], wind_halo[1]))):
        v = lon_weights(c, h, lane)
        for m in range(13):
            lonw[n, m] = v[m]
    hi = lax.Precision.HIGHEST
    i, j = iota((128, 128), 0), iota((128, 128), 1)
    order = jnp.where(((i & 7) * 16 + (i >> 3)) == j, 1.0, 0.0)
    by_level = jnp.dot(order, mixing[...], precision=hi, preferred_element_type=F32)
    spread = jnp.where((iota((16, 128), 1) >> 3) == iota((16, 128), 0), 1.0, 0.0)
    matrix = jnp.dot(by_level, spread, precision=hi, preferred_element_type=F32)
    matrix = jnp.where((i & 7) == (j & 7), matrix, 0.0)
    column[...] = jnp.broadcast_to(by_level[:, 0:1], (128, 128))

    def mix(t, carry):
        out[t] = jnp.dot(matrix, swept[t], precision=hi, preferred_element_type=F32)
        return carry

    lax.fori_loop(0, 16, mix, 0)


def emit_kernel(got, mixed, lonw, latw, column, out, grid):
    lane = iota((8, 128), 1)
    sub = iota((8, 128), 0)
    spots = got[pl.ds(9, 128, stride=ROWS), :].T.astype(jnp.int32)
    row_of, col_of = spots >> 7, spots & 127

    def operands(b):
        x = got[pl.ds(b, 128, stride=ROWS), :].T
        high = x.astype(BF16).astype(F32)
        low = x - high
        highs, lows = [], []
        for s in range(8):
            here = row_of[8 * b + s : 8 * b + s + 1, :] == sub

            def spread(y):
                y = jnp.broadcast_to(y[16 * s : 16 * s + 16][:, None, :], (16, 8, 128))
                return jnp.where(here[None], y, 0.0).reshape(128, 128).astype(BF16)

            highs.append(spread(high))
            lows.append(spread(low))
        return jnp.concatenate(highs, 1), jnp.concatenate(lows, 1)

    def columns(b, first, count):
        target = iota((count, 128), 0) + first
        parts = [
            jnp.where(col_of[8 * b + s : 8 * b + s + 1, :] == target, 1.0, 0.0) for s in range(8)
        ]
        whole = jnp.concatenate(parts, 1)
        pieces = []
        if first:
            pieces.append(jnp.zeros((first, 1024), F32))
        pieces.append(whole)
        if first + count < 128:
            pieces.append(jnp.zeros((128 - first - count, 1024), F32))
        return jnp.concatenate(pieces, 0).astype(BF16) if len(pieces) > 1 else whole.astype(BF16)

    def place(b, first, count):
        high, low = operands(b)
        where = columns(b, first, count)
        return lax.dot_general(high, where, NT, preferred_element_type=F32) + lax.dot_general(
            low, where, NT, preferred_element_type=F32
        )

    for n in range(3):
        grid[n, 0] = place(3 * n + 1, 0, 128)
        grid[n, 1] = place(3 * n, 120, 8) + place(3 * n + 2, 0, 8)

    def tracer(t, carry):
        rows = pl.ds(8 * t, 8)
        swept = []
        for n in range(3):
            v = [lonw[n, m] for m in range(13)]
            h = grid[n, 1, rows, :]
            swept.append(apply13(v, grid[n, 0, rows, :], h, h, 1, lane))
        v = [latw[0, m] for m in range(13)]
        e = apply13(v, swept[1], swept[0], swept[2], 0, sub)
        for k in range(16):
            out[t, k] = mixed[t, pl.ds(8 * k, 8), :] + column[pl.ds(8 * k, 8), :] * e
        return carry

    lax.fori_loop(0, 16, tracer, 0)


def call(kernel, ins, outs, scratch=(), smem=0, cost=None):
    return pl.pallas_call(
        kernel,
        out_shape=[jax.ShapeDtypeStruct(s, F32) for s in outs],
        in_specs=[sspec()] * smem + [vspec()] * (len(ins) - smem),
        out_specs=[vspec()] * len(outs),
        scratch_shapes=[VM(s, F32) for s in scratch],
        compiler_params=PARAMS,
        cost_estimate=cost,
    )(*ins)


def pairs(count, first):
    out = []
    for i in range(first, count - 1 + first, 2):
        j = (i + 1) % count
        if j > i or first == 1:
            out += [(i, j), (j, i)]
    return out


def on_device(
    features, land_tile, land_spot, w_in, b_in, w_mid, b_mid, w_out, tracers, zonal_wind, meridional_wind, mixing
):
    ids = jnp.stack([lax.axis_index("lat"), lax.axis_index("lon")]).astype(jnp.int32)
    pack_a, pack_b = call(pack_kernel, (ids, tracers, zonal_wind), [(17, 8, 128)] * 2, smem=1)
    lon_a = [(i, i ^ 1) for i in range(16)]
    lon_b = [(i, (i + 1) % 16 if i & 1 else (i - 1) % 16) for i in range(16)]
    lat_a = [(i, i ^ 1) for i in range(8)]
    lat_b = [(i, i + 1 if i & 1 else i - 1) for i in range(1, 7)]
    halo_b = lax.ppermute(pack_b, "lon", lon_b)
    halo_a = lax.ppermute(pack_a, "lon", lon_a)
    cells = features.shape[0]
    (message,) = call(
        flux_kernel,
        (
            features.T,
            land_tile.reshape(1, cells),
            land_spot.reshape(1, cells),
            w_in,
            b_in.reshape(1, -1),
            w_mid,
            b_mid.reshape(1, -1),
            w_out.T,
        ),
        [(128 * ROWS, 128)],
    )
    got = lax.all_to_all(
        message.reshape(128, 1, ROWS * 128), ("lat", "lon"), split_axis=0, concat_axis=0, tiled=True
    ).reshape(128 * ROWS, 128)
    state, row_a, row_b = call(
        lon_kernel,
        (ids, tracers, zonal_wind, meridional_wind, halo_a, halo_b),
        [(16, 16, 8, 128), (LATMSG, 8, 128), (LATMSG, 8, 128)],
        smem=1,
    )
    rows_a = lax.ppermute(row_a, "lat", lat_a)
    rows_b = lax.ppermute(row_b, "lat", lat_b)
    mixed, lonw, latw, column = call(
        lat_kernel,
        (
            ids,
            state,
            zonal_wind,
            meridional_wind,
            rows_a,
            rows_b,
            halo_a,
            halo_b,
            mixing.reshape(128, 16),
        ),
        [(16, 128, 128), (3, 13, 8, 128), (16, 13, 8, 128), (128, 128)],
        scratch=[(16, 128, 128)],
        smem=1,
    )
    (out,) = call(
        emit_kernel,
        (got, mixed, lonw, latw, column),
        [(16, 16, 8, 128)],
        scratch=[(3, 2, 128, 128)],
    )
    return out


def solution(mesh):
    placed = (
        P(("lat", "lon"), None),
        P(("lat", "lon"), None),
        P(("lat", "lon")),
        P(),
        P(),
        P(),
        P(),
        P(),
        P(None, None, "lat", "lon"),
        P(None, "lat", "lon"),
        P(None, "lat", "lon"),
        P("lat", None, None),
    )
    return jax.shard_map(
        on_device,
        mesh=mesh,
        in_specs=placed,
        out_specs=P(None, None, "lat", "lon"),
        check_vma=False,
    )
```

time: 173 us -> 80.6 us (0.47)
  the two profiles are of different devices: /device:TPU:2 before, /device:TPU:31 now
where the time goes in v1:
time: 80.6 us; the launch traced here: 80.1 us
  Pallas kernels  31.3 us (39%)
  waiting for transfers between devices  22.6 us (28%)
  starting transfers between devices  14.4 us (18%)
  local copies, waits for them, and re-layouts  11.5 us (14%)
    pallas_call x5, Pallas kernels, call(): pl.pallas_call(kernel, out_shape=[jax.ShapeDtypeStruct(s, F32) for s in o...  31.3 us
    unnamed x44, local copies, waits for them, and re-layouts  11.5 us
    ppermute x1, waiting for transfers between devices, on_device(): rows_a = lax.ppermute(row_a, 'lat', lat_a)  10.7 us
    all_to_all x1, starting transfers between devices, on_device(): lax.all_to_all(message.reshape(128, 1, ROWS * 128), ('lat', 'lon'), split...  6.86 us
    ppermute x1, waiting for transfers between devices, on_device(): halo_b = lax.ppermute(pack_b, 'lon', lon_b)  6.44 us
    ppermute x1, waiting for transfers between devices, on_device(): rows_b = lax.ppermute(row_b, 'lat', lat_b)  5.33 us
    ppermute x1, starting transfers between devices, on_device(): rows_b = lax.ppermute(row_b, 'lat', lat_b)  4.4 us
    ppermute x1, starting transfers between devices, on_device(): rows_a = lax.ppermute(row_a, 'lat', lat_a)  1.64 us
  transfers between devices with their start and end apart: 5, of which 4 were waited for; matrix products, arithmetic and copies ran while one was open for 0% of the time, Pallas kernels for 12%

profile of v1, /device:TPU:31, one launch (start us, length us, event | category | flops | bytes accessed | tf_op | source)
XLA Modules:
  0.0 80.1 jit_solution(6111402881513955899)
XLA Ops:
  0.0 0.1 pad_add_fusion.ids
  0.1 0.0 copy-start
  0.1 1.2 %copy-done = f32[16,16,8,128]{3,2,1,0:T(8,128)S(1)} copy-done((f32[16,16,8,128]{3,2,1,0:T(8,128)S(1)}, f32[16,16,8,128]{3,2,1,0:T(8,128)}, u32[]{:S(2)}) %copy-start) | copy-done | bytes 1048600
  1.3 0.0 copy-start.7
  1.3 0.8 %copy-done.7 = f32[16,8,128]{2,1,0:T(8,128)S(1)} copy-done((f32[16,8,128]{2,1,0:T(8,128)S(1)}, f32[16,8,128]{2,1,0:T(8,128)}, u32[]{:S(2)}) %copy-start.7) | copy-done | bytes 65560
  2.1 0.0 copy-start.11
  2.1 2.0 %shard_map.119 = (f32[17,8,128]{2,1,0:T(8,128)S(1)}, f32[17,8,128]{2,1,0:T(8,128)S(1)}) custom-call(s32[2]{0:T(128)S(1)} %pad_add_fusion.ids, f32[16,16,8,128]{3,2,1,0:T(8,128)S(1)} %copy-done, f32[16,8,128]{2,1,0:T(8,128)S(1)} %copy-done.7), custom_call_target="tpu_custom_call" | custom-call | tf_op jit(solution)/shard_map/pallas_call | solution.py:369
  4.1 0.7 collective-permute-start
  4.8 0.0 copy-start.13
  4.8 0.0 copy-start.14
  4.8 0.8 collective-permute-start.1
  5.6 0.1 collective-permute-done.halo_a.zonal_halo_a
  5.7 6.4 %collective-permute-done.1.halo_b.zonal_halo_b = f32[17,8,128]{2,1,0:T(8,128)S(1)} collective-permute-done((f32[17,8,128]{2,1,0:T(8,128)S(1)}, f32[17,8,128]{2,1,0:T(8,128)S(1)}, u32[]{:S(2)}, u32[]{:S(2)}) %collective-permute-start.1) | collective-permute-done | bytes 69664 | tf_op jit(solution)/shard_map/ppermute | solution.py:398
  12.2 0.0 copy-done.11
  12.2 0.0 copy-start.9
  12.2 0.0 copy-start.16
  12.2 0.0 copy-start.21
  12.2 15.0 %shard_map.120 = (f32[16,16,8,128]{3,2,1,0:T(8,128)S(1)}, f32[206,8,128]{2,1,0:T(8,128)}, f32[206,8,128]{2,1,0:T(8,128)}) custom-call(s32[2]{0:T(128)S(1)} %pad_add_fusion.ids, f32[16,16,8,128]{3,2,1,0:T(8,128)S(1)} %copy-done, f32[16,8,128]{2,1,0:T(8,128)S(1)} %copy-done.7, f32[16,8,128]{2,1,0:T(8,128)S(1)} %copy-done.11, ...), custom_call_target="tpu_custom_call" | custom-call | tf_op jit(solution)/shard_map/pallas_call | solution.py:369
  27.2 0.0 copy-done.9
  27.2 0.0 copy-start.17
  27.2 1.6 %collective-permute-start.2 = (f32[206,8,128]{2,1,0:T(8,128)}, f32[206,8,128]{2,1,0:T(8,128)S(1)}, u32[]{:S(2)}, u32[]{:S(2)}) collective-permute-start(f32[206,8,128]{2,1,0:T(8,128)} %get-tuple-element.17), channel_id=1, source_target_pairs={{0,16},{16,0},{32,48},{48,32},{64,80},{80,64},{96,112},{112,96},{1... | collective-permute-start | bytes 2531336 | tf_op jit(solution)/shard_map/ppermute | solution.py:424
  28.9 4.4 %collective-permute-start.3 = (f32[206,8,128]{2,1,0:T(8,128)}, f32[206,8,128]{2,1,0:T(8,128)S(1)}, u32[]{:S(2)}, u32[]{:S(2)}) collective-permute-start(f32[206,8,128]{2,1,0:T(8,128)} %get-tuple-element.18), channel_id=1, source_target_pairs={{16,32},{32,16},{48,64},{64,48},{80,96},{96,80},{17,33},{33,17},{4... | collective-permute-start | bytes 2531336 | tf_op jit(solution)/shard_map/ppermute | solution.py:425
  33.3 0.0 copy-start.19
  33.3 0.0 copy-start.18
  33.3 0.0 copy-start.20
  33.3 0.0 copy-done.13
  33.3 0.0 copy-done.14
  33.3 0.0 copy-done.16
  33.3 0.0 copy-done.21
  33.4 0.0 copy-done.17
  33.4 0.6 copy-done.19
  34.0 0.0 copy-done.18
  34.0 0.0 copy-done.20
  34.0 1.9 %shard_map.118 = f32[1280,128]{1,0:T(8,128)} custom-call(bf16[64,512]{1,0:T(8,128)(2,1)S(1)} %bitcast.12, s32[1,512]{1,0:T(1,128)S(1)} %bitcast.15, s32[1,512]{1,0:T(1,128)S(1)} %bitcast.16, bf16[64,256]{1,0:T(8,128)(2,1)S(1)} %copy-done.16, f32[1,256]{1,0:T(1,128)S(1)} %bitcast.17, bf16[256,256]{1,0:T(8,128)(2,1)S(1)} %copy-done.13, f32[1,256]{1,0:T(1,128)S(1)} %bitcast.18, ...), custom_call_target="tpu_custom_call" | custom-call | tf_op jit(solution)/shard_map/pallas_call | solution.py:369
  35.9 0.0 copy-start.8
  35.9 6.9 %all-to-all-start = ((f32[128,1,1280]{2,1,0:T(1,128)}), f32[128,1,1280]{2,1,0:T(1,128)S(1)}, u32[]{:S(2)}, u32[]{:S(2)}) async-start(f32[128,1,1280]{2,1,0:T(1,128)} %bitcast.6), calls=%async_computation | async-start | bytes 1310720 | tf_op jit(solution)/shard_map/all_to_all | solution.py:415
  42.8 10.7 %collective-permute-done.2.halo_a = f32[206,8,128]{2,1,0:T(8,128)S(1)} collective-permute-done((f32[206,8,128]{2,1,0:T(8,128)}, f32[206,8,128]{2,1,0:T(8,128)S(1)}, u32[]{:S(2)}, u32[]{:S(2)}) %collective-permute-start.2) | collective-permute-done | bytes 843808 | tf_op jit(solution)/shard_map/ppermute | solution.py:424
  53.5 0.0 copy-start.3
  53.5 0.9 %copy-done.3 = f32[206,8,128]{2,1,0:T(8,128)} copy-done((f32[206,8,128]{2,1,0:T(8,128)}, f32[206,8,128]{2,1,0:T(8,128)S(1)}, u32[]{:S(2)}) %copy-start.3) | copy-done | bytes 843800
  54.4 5.3 %collective-permute-done.3.halo_b = f32[206,8,128]{2,1,0:T(8,128)S(1)} collective-permute-done((f32[206,8,128]{2,1,0:T(8,128)}, f32[206,8,128]{2,1,0:T(8,128)S(1)}, u32[]{:S(2)}, u32[]{:S(2)}) %collective-permute-start.3) | collective-permute-done | bytes 843808 | tf_op jit(solution)/shard_map/ppermute | solution.py:425
  59.7 0.0 copy-start.5
  59.7 0.9 %copy-done.5 = f32[206,8,128]{2,1,0:T(8,128)} copy-done((f32[206,8,128]{2,1,0:T(8,128)}, f32[206,8,128]{2,1,0:T(8,128)S(1)}, u32[]{:S(2)}) %copy-start.5) | copy-done | bytes 843800
  60.6 0.0 copy-done.8
  60.7 0.0 copy-start.4
  60.7 1.2 %copy-done.4 = f32[206,8,128]{2,1,0:T(8,128)S(1)} copy-done((f32[206,8,128]{2,1,0:T(8,128)S(1)}, f32[206,8,128]{2,1,0:T(8,128)}, u32[]{:S(2)}) %copy-start.4) | copy-done | bytes 843800
  61.8 0.0 copy-start.6
  61.8 1.2 %copy-done.6 = f32[206,8,128]{2,1,0:T(8,128)S(1)} copy-done((f32[206,8,128]{2,1,0:T(8,128)S(1)}, f32[206,8,128]{2,1,0:T(8,128)}, u32[]{:S(2)}) %copy-start.6) | copy-done | bytes 843800
  63.0 0.0 copy-start.10
  63.0 0.9 %copy-done.10 = f32[17,8,128]{2,1,0:T(8,128)S(1)} copy-done((f32[17,8,128]{2,1,0:T(8,128)S(1)}, f32[17,8,128]{2,1,0:T(8,128)}, u32[]{:S(2)}) %copy-start.10) | copy-done | bytes 69656
  63.8 0.0 copy-start.12
  63.8 0.8 %copy-done.12 = f32[16,8,128]{2,1,0:T(8,128)S(1)} copy-done((f32[16,8,128]{2,1,0:T(8,128)S(1)}, f32[16,8,128]{2,1,0:T(8,128)}, u32[]{:S(2)}) %copy-start.12) | copy-done | bytes 65560
  64.7 0.0 copy-start.15
  64.7 0.8 %copy-done.15 = f32[8,16,16]{2,1,0:T(8,128)S(1)} copy-done((f32[8,16,16]{2,1,0:T(8,128)S(1)}, f32[8,16,16]{2,1,0:T(8,128)}, u32[]{:S(2)}) %copy-start.15) | copy-done | bytes 8216
  65.5 7.7 %shard_map.121 = (f32[16,128,128]{2,1,0:T(8,128)S(1)}, f32[3,13,8,128]{3,2,1,0:T(8,128)S(1)}, f32[16,13,8,128]{3,2,1,0:T(8,128)S(1)}, f32[128,128]{1,0:T(8,128)S(1)}) custom-call(s32[2]{0:T(128)S(1)} %pad_add_fusion.ids, f32[16,16,8,128]{3,2,1,0:T(8,128)S(1)} %get-tuple-element.16.state, f32[16,8,128]{2,1,0:T(8,128)S(1)} %copy-done.8, ...), custom_call_target="tpu_custom_call" | custom-call | tf_op jit(solution)/shard_map/pallas_call | solution.py:369
  73.3 0.0 copy-start.1
  73.3 0.9 %copy-done.1 = f32[16,13,8,128]{3,2,1,0:T(8,128)} copy-done((f32[16,13,8,128]{3,2,1,0:T(8,128)}, f32[16,13,8,128]{3,2,1,0:T(8,128)S(1)}, u32[]{:S(2)}) %copy-start.1) | copy-done | bytes 851992
  74.2 0.0 all-to-all-done
  74.2 0.0 copy-start.2
  74.2 1.2 %copy-done.2 = f32[16,13,8,128]{3,2,1,0:T(8,128)S(1)} copy-done((f32[16,13,8,128]{3,2,1,0:T(8,128)S(1)}, f32[16,13,8,128]{3,2,1,0:T(8,128)}, u32[]{:S(2)}) %copy-start.2) | copy-done | bytes 851992
  75.3 4.7 %shard_map.122 = f32[16,16,8,128]{3,2,1,0:T(8,128)} custom-call(f32[1280,128]{1,0:T(8,128)S(1)} %bitcast.11, f32[16,128,128]{2,1,0:T(8,128)S(1)} %get-tuple-element.19.mixed, f32[3,13,8,128]{3,2,1,0:T(8,128)S(1)} %get-tuple-element.20.lonw, f32[16,13,8,128]{3,2,1,0:T(8,128)S(1)} %copy-done.2, f32[128,128]{1,0:T(8,128)S(1)} %get-tuple-element.22.column), custom_call_target="tpu_custom_call" | custom-call | tf_op jit(solution)/shard_map/pallas_call | solution.py:369
Async XLA Ops:
  0.1 1.2 %copy-start = (f32[16,16,8,128]{3,2,1,0:T(8,128)S(1)}, f32[16,16,8,128]{3,2,1,0:T(8,128)}, u32[]{:S(2)}) copy-start(f32[16,16,8,128]{3,2,1,0:T(8,128)} %tracers.3) | copy-start | bytes 3145732
  1.3 0.8 %copy-start.7 = (f32[16,8,128]{2,1,0:T(8,128)S(1)}, f32[16,8,128]{2,1,0:T(8,128)}, u32[]{:S(2)}) copy-start(f32[16,8,128]{2,1,0:T(8,128)} %zonal.5) | copy-start | bytes 196612
  2.1 10.0 %copy-start.11 = (f32[16,8,128]{2,1,0:T(8,128)S(1)}, f32[16,8,128]{2,1,0:T(8,128)}, u32[]{:S(2)}) copy-start(f32[16,8,128]{2,1,0:T(8,128)} %merid.3) | copy-start | bytes 196612
  4.1 1.6 %collective-permute-start = (f32[17,8,128]{2,1,0:T(8,128)S(1)}, f32[17,8,128]{2,1,0:T(8,128)S(1)}, u32[]{:S(2)}, u32[]{:S(2)}) collective-permute-start(f32[17,8,128]{2,1,0:T(8,128)S(1)} %get-tuple-element.14), channel_id=1, source_target_pairs={{0,1},{1,0},{2,3},{3,2},{4,5},{5,4},{6,7},{7,6},{8,9},{9,8},{10,11... | collective-permute-start | bytes 208904 | tf_op jit(solution)/shard_map/ppermute | solution.py:399
  4.8 28.5 %copy-start.13 = (bf16[256,256]{1,0:T(8,128)(2,1)S(1)}, bf16[256,256]{1,0:T(8,128)(2,1)}, u32[]{:S(2)}) copy-start(bf16[256,256]{1,0:T(8,128)(2,1)} %w_mid.1) | copy-start | bytes 393220
  4.8 28.5 %copy-start.14 = (bf16[512,64]{0,1:T(8,128)(2,1)S(1)}, bf16[512,64]{0,1:T(8,128)(2,1)}, u32[]{:S(2)}) copy-start(bf16[512,64]{0,1:T(8,128)(2,1)} %param.12) | copy-start | bytes 196612
  4.8 7.3 %collective-permute-start.1 = (f32[17,8,128]{2,1,0:T(8,128)S(1)}, f32[17,8,128]{2,1,0:T(8,128)S(1)}, u32[]{:S(2)}, u32[]{:S(2)}) collective-permute-start(f32[17,8,128]{2,1,0:T(8,128)S(1)} %get-tuple-element.15), channel_id=1, source_target_pairs={{0,15},{1,2},{2,1},{3,4},{4,3},{5,6},{6,5},{7,8},{8,7},{9,10},{10,... | collective-permute-start | bytes 208904 | tf_op jit(solution)/shard_map/ppermute | solution.py:398
  12.2 15.0 %copy-start.9 = (f32[17,8,128]{2,1,0:T(8,128)}, f32[17,8,128]{2,1,0:T(8,128)S(1)}, u32[]{:S(2)}) copy-start(f32[17,8,128]{2,1,0:T(8,128)S(1)} %collective-permute-done.1.halo_b.zonal_halo_b) | copy-start | bytes 208900
  12.2 21.2 %copy-start.16 = (bf16[64,256]{1,0:T(8,128)(2,1)S(1)}, bf16[64,256]{1,0:T(8,128)(2,1)}, u32[]{:S(2)}) copy-start(bf16[64,256]{1,0:T(8,128)(2,1)} %w_in.1) | copy-start | bytes 98308
  12.2 21.2 %copy-start.21 = (f32[256]{0:T(256)S(1)}, f32[256]{0:T(256)}, u32[]{:S(2)}) copy-start(f32[256]{0:T(256)} %param.18) | copy-start | bytes 3076
  27.2 6.1 %copy-start.17 = (bf16[256,16]{0,1:T(8,128)(2,1)S(1)}, bf16[256,16]{0,1:T(8,128)(2,1)}, u32[]{:S(2)}) copy-start(bf16[256,16]{0,1:T(8,128)(2,1)} %param.19) | copy-start | bytes 24580
  27.2 26.3 %collective-permute-start.2 = (f32[206,8,128]{2,1,0:T(8,128)}, f32[206,8,128]{2,1,0:T(8,128)S(1)}, u32[]{:S(2)}, u32[]{:S(2)}) collective-permute-start(f32[206,8,128]{2,1,0:T(8,128)} %get-tuple-element.17), channel_id=1, source_target_pairs={{0,16},{16,0},{32,48},{48,32},{64,80},{80,64},{96,112},{112,96},{1... | collective-permute-start | bytes 2531336 | tf_op jit(solution)/shard_map/ppermute | solution.py:424
  28.9 30.9 %collective-permute-start.3 = (f32[206,8,128]{2,1,0:T(8,128)}, f32[206,8,128]{2,1,0:T(8,128)S(1)}, u32[]{:S(2)}, u32[]{:S(2)}) collective-permute-start(f32[206,8,128]{2,1,0:T(8,128)} %get-tuple-element.18), channel_id=1, source_target_pairs={{16,32},{32,16},{48,64},{64,48},{80,96},{96,80},{17,33},{33,17},{4... | collective-permute-start | bytes 2531336 | tf_op jit(solution)/shard_map/ppermute | solution.py:425
  33.3 0.7 copy-start.19
  33.3 0.7 copy-start.18
  33.3 0.7 copy-start.20
  35.9 24.8 %copy-start.8 = (f32[16,8,128]{2,1,0:T(8,128)S(1)}, f32[16,8,128]{2,1,0:T(8,128)}, u32[]{:S(2)}) copy-start(f32[16,8,128]{2,1,0:T(8,128)} %zonal.5) | copy-start | bytes 196612
  35.9 38.3 %all-to-all-start = ((f32[128,1,1280]{2,1,0:T(1,128)}), f32[128,1,1280]{2,1,0:T(1,128)S(1)}, u32[]{:S(2)}, u32[]{:S(2)}) async-start(f32[128,1,1280]{2,1,0:T(1,128)} %bitcast.6), calls=%async_computation | async-start | bytes 1310720 | tf_op jit(solution)/shard_map/all_to_all | solution.py:415
  53.5 0.9 %copy-start.3 = (f32[206,8,128]{2,1,0:T(8,128)}, f32[206,8,128]{2,1,0:T(8,128)S(1)}, u32[]{:S(2)}) copy-start(f32[206,8,128]{2,1,0:T(8,128)S(1)} %collective-permute-done.2.halo_a) | copy-start | bytes 2531332
  59.7 0.9 %copy-start.5 = (f32[206,8,128]{2,1,0:T(8,128)}, f32[206,8,128]{2,1,0:T(8,128)S(1)}, u32[]{:S(2)}) copy-start(f32[206,8,128]{2,1,0:T(8,128)S(1)} %collective-permute-done.3.halo_b) | copy-start | bytes 2531332
  60.7 1.2 %copy-start.4 = (f32[206,8,128]{2,1,0:T(8,128)S(1)}, f32[206,8,128]{2,1,0:T(8,128)}, u32[]{:S(2)}) copy-start(f32[206,8,128]{2,1,0:T(8,128)} %copy-done.3) | copy-start | bytes 2531332
  61.8 1.2 %copy-start.6 = (f32[206,8,128]{2,1,0:T(8,128)S(1)}, f32[206,8,128]{2,1,0:T(8,128)}, u32[]{:S(2)}) copy-start(f32[206,8,128]{2,1,0:T(8,128)} %copy-done.5) | copy-start | bytes 2531332
  63.0 0.9 %copy-start.10 = (f32[17,8,128]{2,1,0:T(8,128)S(1)}, f32[17,8,128]{2,1,0:T(8,128)}, u32[]{:S(2)}) copy-start(f32[17,8,128]{2,1,0:T(8,128)} %copy-done.9) | copy-start | bytes 208900
  63.8 0.8 %copy-start.12 = (f32[16,8,128]{2,1,0:T(8,128)S(1)}, f32[16,8,128]{2,1,0:T(8,128)}, u32[]{:S(2)}) copy-start(f32[16,8,128]{2,1,0:T(8,128)} %merid.3) | copy-start | bytes 196612
  64.7 0.8 %copy-start.15 = (f32[8,16,16]{2,1,0:T(8,128)S(1)}, f32[8,16,16]{2,1,0:T(8,128)}, u32[]{:S(2)}) copy-start(f32[8,16,16]{2,1,0:T(8,128)} %param.23) | copy-start | bytes 24580
  73.3 0.9 %copy-start.1 = (f32[16,13,8,128]{3,2,1,0:T(8,128)}, f32[16,13,8,128]{3,2,1,0:T(8,128)S(1)}, u32[]{:S(2)}) copy-start(f32[16,13,8,128]{3,2,1,0:T(8,128)S(1)} %get-tuple-element.21.latw) | copy-start | bytes 2555908
  74.2 1.2 %copy-start.2 = (f32[16,13,8,128]{3,2,1,0:T(8,128)S(1)}, f32[16,13,8,128]{3,2,1,0:T(8,128)}, u32[]{:S(2)}) copy-start(f32[16,13,8,128]{3,2,1,0:T(8,128)} %copy-done.1) | copy-start | bytes 2555908

commit v2 on v1

v2 whole, which is shorter than its diff:
```python
import jax
import jax.numpy as jnp
from jax import lax
from jax.experimental import pallas as pl
from jax.experimental.pallas import tpu as pltpu
from jax.sharding import PartitionSpec as P

F32 = jnp.float32
BF16 = jnp.bfloat16
NT = (((1,), (1,)), ((), ()))
TN = (((0,), (0,)), ((), ()))
ROWS = 10
LATMSG = 17 * 12 + 3
VM = pltpu.VMEM
PARAMS = pltpu.CompilerParams(vmem_limit_bytes=12 * 1024 * 1024)


def vspec():
    return pl.BlockSpec(memory_space=VM)


def iota(shape, dim):
    return lax.broadcasted_iota(jnp.int32, shape, dim)


def face_weights(c):
    pos = c >= 0
    w = jnp.abs(c)
    al = 0.5 * w * w
    be = 3.0 * al - 2.0 * al * w
    p = w - al - be
    g = al - be
    h = 2.0 * be
    p = jnp.where(pos, p, -p)
    zero = jnp.zeros_like(c)
    gp = jnp.where(pos, g, zero)
    gm = jnp.where(pos, zero, -g)
    hp = jnp.where(pos, h, zero)
    hm = jnp.where(pos, zero, -h)
    a, b = 7.0 / 12.0, 1.0 / 12.0
    return [
        -b * gp,
        a * gp - b * p,
        a * (p + gp) - b * gm + hp,
        a * (p + gm) - b * gp + hm,
        a * gm - b * p,
        -b * gm,
    ]


def step_weights(f, f_before):
    out = []
    for m in range(-3, 4):
        v = None
        if m <= 2:
            v = f_before[m + 3]
        if m >= -2:
            v = -f[m + 2] if v is None else v - f[m + 2]
        if m == 0:
            v = v + 1.0
        out.append(v)
    return out


def shifted(q, low, high, s, axis, pos):
    n = q.shape[axis]
    if s == 0:
        return q
    if s > 0:
        return pltpu.roll(jnp.where(pos < s, high, q), n - s, axis)
    return pltpu.roll(jnp.where(pos >= n + s, low, q), -s, axis)


def double_weights(w, w_low, w_high, axis, pos):
    out = [None] * 13
    for a in range(-3, 4):
        for b in range(-3, 4):
            v = w[a + 3] * shifted(w[b + 3], w_low[b + 3], w_high[b + 3], a, axis, pos)
            out[a + b + 6] = v if out[a + b + 6] is None else out[a + b + 6] + v
    return out


def zonal_weights(wind, out):
    def block(b, carry):
        f = face_weights(wind[pl.ds(8 * b + 5, 8), :])
        before = face_weights(wind[pl.ds(8 * b + 4, 8), :])
        for m, w in enumerate(step_weights(f, before)):
            out[m, pl.ds(pl.multiple_of(8 * b, 8), 8), :] = w
        return carry

    lax.fori_loop(0, 17, block, 0)


def zonal_steps_unrolled(weights, first, second):
    def total(terms):
        while len(terms) > 1:
            terms = [x + y for x, y in zip(terms[::2], terms[1::2])] + ([terms[-1]] if len(terms) & 1 else [])
        return terms[0]

    for b in range(17):
        second[8 * b : 8 * b + 8] = total(
            [weights[m, 8 * b : 8 * b + 8, :] * first[8 * b + 2 + m : 8 * b + 10 + m] for m in range(7)]
        )
    for b in range(16):
        first[8 * b + 8 : 8 * b + 16] = total(
            [weights[m, 8 * b + 3 : 8 * b + 11, :] * second[8 * b + m : 8 * b + 8 + m] for m in range(7)]
        )


def zonal_steps(weights, first, second, count):
    def one(b, carry):
        w = [weights[m, pl.ds(pl.multiple_of(8 * b, 8), 8), :] for m in range(7)]
        for t in range(count):
            v = w[0] * first[t, pl.ds(8 * b + 2, 8), :]
            for m in range(1, 7):
                v = v + w[m] * first[t, pl.ds(8 * b + 2 + m, 8), :]
            second[t, pl.ds(pl.multiple_of(8 * b, 8), 8), :] = v
        return carry

    lax.fori_loop(0, 17, one, 0)

    def two(b, carry):
        w = [weights[m, pl.ds(8 * b + 3, 8), :] for m in range(7)]
        for t in range(count):
            v = w[0] * second[t, pl.ds(8 * b, 8), :]
            for m in range(1, 7):
                v = v + w[m] * second[t, pl.ds(8 * b + m, 8), :]
            first[t, pl.ds(pl.multiple_of(8 * b + 8, 8), 8), :] = v
        return carry

    lax.fori_loop(0, 16, two, 0)


def lat_weights(c, low, high, sub):
    f, fl, fh = face_weights(c), face_weights(low), face_weights(high)
    before = [shifted(x, y, y, -1, 0, sub) for x, y in zip(f, fl)]
    low_before = [shifted(y, y, y, -1, 0, sub) for y in fl]
    high_before = [shifted(y, x, x, -1, 0, sub) for x, y in zip(f, fh)]
    w = step_weights(f, before)
    wl = step_weights(fl, low_before)
    wh = step_weights(fh, high_before)
    return double_weights(w, wl, wh, 0, sub)


def pack_kernel(ids, tracers_hbm, zonal_hbm, out_a, out_b, turned, tracers, zonal, sems):
    odd = (ids[1] & 1) == 1
    chunks = [(zonal_hbm, zonal)]
    chunks += [(tracers_hbm.at[pl.ds(4 * n, 4)], tracers.at[pl.ds(4 * n, 4)]) for n in range(4)]
    copies = load(chunks, sems)

    def put(t, x):
        x = x.T
        turned[t] = x
        left, right = x[0:8], x[120:128]
        out_a[t] = jnp.where(odd, left, right)
        out_b[t] = jnp.where(odd, right, left)

    copies[0].wait()
    put(16, zonal[...])
    for n in range(4):
        copies[n + 1].wait()
        for t in range(4 * n, 4 * n + 4):
            put(t, tracers[t])


def flux_kernel(*refs):
    out, sems = refs[8], refs[17]
    feat, tile, spot, w_in, b_in, w_mid, b_mid, w_out = refs[9:17]
    for c in load(list(zip(refs[:8], refs[9:17])), sems):
        c.wait()

    def silu(v):
        return (v / (1.0 + jnp.exp(-v))).astype(BF16)

    first = silu(lax.dot_general(feat[...], w_in[...], TN, preferred_element_type=F32) + b_in[...])
    second = silu(jnp.dot(first, w_mid[...], preferred_element_type=F32) + b_mid[...])
    flux = lax.dot_general(w_out[...], second, NT, preferred_element_type=F32)
    cells = flux.shape[1]
    member = iota((128, cells), 0) == tile[...]
    member32 = jnp.where(member, 1.0, 0.0)
    member16 = member32.astype(BF16)
    upper = jnp.where(iota((cells, cells), 0) < iota((cells, cells), 1), 1.0, 0.0).astype(BF16)
    earlier = jnp.dot(member16, upper, preferred_element_type=F32)
    slot = jnp.sum(member32 * earlier, axis=0, keepdims=True).astype(jnp.int32)
    high = flux.astype(BF16).astype(F32)
    low = flux - high
    zero = jnp.zeros_like(flux)
    rows_high = jnp.concatenate([jnp.where(slot == s, high, zero) for s in range(8)], 0)
    rows_low = jnp.concatenate([jnp.where(slot == s, low, zero) for s in range(8)], 0)
    sent = lax.dot_general(
        member16, rows_high.astype(BF16), NT, preferred_element_type=F32
    ) + lax.dot_general(member16, rows_low.astype(BF16), NT, preferred_element_type=F32)
    here = (iota((128, cells), 0) & 7) == slot
    places = spot[...]
    coarse = jnp.where(here, (places >> 4) << 4, 0).astype(F32).astype(BF16)
    fine = jnp.where(here, places & 15, 0).astype(F32).astype(BF16)
    spots = lax.dot_general(member16, coarse, NT, preferred_element_type=F32) + lax.dot_general(
        member16, fine, NT, preferred_element_type=F32
    )
    row = iota((128, 128), 0)
    group = iota((128, 128), 1) >> 3

    def beside(x, dn):
        if dn == 0:
            return x
        if dn == 1:
            return jnp.where((row & 15) == 15, pltpu.roll(x, 15, 0), pltpu.roll(x, 127, 0))
        return jnp.where((row & 15) == 0, pltpu.roll(x, 113, 0), pltpu.roll(x, 1, 0))

    def above(x, dl):
        pad = jnp.zeros((16, 128), F32)
        if dl == 0:
            return x
        if dl == 1:
            return jnp.concatenate([x[16:], pad], 0)
        return jnp.concatenate([pad, x[:-16]], 0)

    places_out = jnp.zeros((128, 128), F32)
    for dn in (-1, 0, 1):
        x, y = beside(sent, dn), beside(spots, dn)
        for dl in (-1, 0, 1):
            b = (dl + 1) * 3 + dn + 1
            out[pl.ds(b, 128, stride=ROWS), :] = above(x, dl)
            places_out = jnp.where(group == b, above(y, dl), places_out)
    out[pl.ds(9, 128, stride=ROWS), :] = places_out


def lon_kernel(
    ids, turned, zonal, merid_hbm, halo_a, halo_b, state, out_a, out_b, wind, weights, first, second, merid, surface, sems
):
    copies = load([(merid_hbm, merid), (zonal.at[pl.ds(0, 8)], surface)], sems)
    odd = (ids[1] & 1) == 1
    odd_lat = (ids[0] & 1) == 1
    sub = iota((8, 128), 0)

    def halo(t):
        a, b = halo_a[t], halo_b[t]
        return jnp.where(odd, a, b), jnp.where(odd, b, a)

    left, right = halo(16)
    wind[0:8], wind[8:136], wind[136:144] = left, turned[16], right
    zonal_weights(wind, weights)
    for t in range(16):
        low, high = halo(t)
        first[t, 0:8], first[t, 8:136], first[t, 136:144] = low, turned[t], high
    zonal_steps(weights, first, second, 16)
    for t in range(16):
        state[t] = first[t, 8:136].T

    def emit(n, up, down):
        out_a[n] = jnp.where(odd_lat, down, up)
        out_b[n] = jnp.where(odd_lat, up, down)

    def pack(t, read):
        for g in range(4):
            q = [read(4 * g + i) for i in range(4)]
            for i in range(3):
                last = pltpu.roll(q[3], 6 - 2 * i, 0)
                emit(t * 12 + g * 3 + i, jnp.where(sub >= 2, q[i], last), jnp.where(sub < 6, q[i], last))

    def body(t, carry):
        pack(t, lambda k: state[t, 8 * k : 8 * k + 8, :])
        return carry

    lax.fori_loop(0, 16, body, 0)
    keep = jnp.logical_or(sub < 7, ids[0] < 7)
    for c in copies:
        c.wait()
    pack(16, lambda k: jnp.where(keep, merid[k], 0.0))
    emit(204, surface[...], surface[...])
    emit(205, left, left)
    emit(206, right, right)


def lat_kernel(
    ids,
    state,
    merid_hbm,
    a_hbm,
    b_hbm,
    edge,
    mixing_hbm,
    out,
    lonw,
    top,
    column,
    swept,
    wide,
    wind,
    latw,
    merid,
    halo_a,
    halo_b,
    mixing,
    sems,
):
    copies = load([(a_hbm, halo_a), (b_hbm, halo_b), (merid_hbm, merid), (mixing_hbm, mixing)], sems)
    odd_lat = (ids[0] & 1) == 1
    sub = iota((8, 128), 0)
    keep = jnp.logical_or(sub < 7, ids[0] < 7)
    hi = lax.Precision.HIGHEST
    i, j = iota((128, 128), 0), iota((128, 128), 1)

    def message(n):
        a, b = halo_a[n], halo_b[n]
        return jnp.where(odd_lat, a, b), jnp.where(odd_lat, b, a)

    def four(t, g):
        got = [message(t * 12 + g * 3 + x) for x in range(3)]
        rolled = [[pltpu.roll(got[x][y], 2 + 2 * x, 0) for x in range(3)] for y in range(2)]
        low = jnp.where(sub < 4, rolled[0][0], jnp.where(sub < 6, rolled[0][1], rolled[0][2]))
        high = jnp.where(sub < 2, rolled[1][0], jnp.where(sub < 4, rolled[1][1], rolled[1][2]))
        return got + [(low, high)]

    def unpack(t, carry):
        for g in range(4):
            for x, (low, high) in enumerate(four(t, g)):
                k = 4 * g + x
                wide[t, k, 0:8], wide[t, k, 8:16], wide[t, k, 16:24] = low, state[t, 8 * k : 8 * k + 8, :], high
        return carry

    spread = jnp.where((j & 7) == i, 1.0, 0.0)

    def level_zero(n):
        wind[n] = jnp.dot(wind[n], spread, precision=hi, preferred_element_type=F32)
        zonal_weights(wind.at[n], lonw.at[n])

    wind[1] = edge[...]
    level_zero(1)
    copies[3].wait()
    order = jnp.where(((i & 7) * 16 + (i >> 3)) == j, 1.0, 0.0)
    by_level = jnp.dot(order, mixing[...], precision=hi, preferred_element_type=F32)
    expand = jnp.where((iota((16, 128), 1) >> 3) == iota((16, 128), 0), 1.0, 0.0)
    matrix = jnp.dot(by_level, expand, precision=hi, preferred_element_type=F32)
    matrix = jnp.where((i & 7) == (j & 7), matrix, 0.0)
    column[...] = jnp.broadcast_to(by_level[:, 0:1], (128, 128))
    for c in copies[:3]:
        c.wait()
    lax.fori_loop(0, 16, unpack, 0)
    for g in range(4):
        for x, (low, high) in enumerate(four(16, g)):
            k = 4 * g + x
            wide[16, k, 0:8], wide[16, k, 8:16], wide[16, k, 16:24] = low, jnp.where(keep, merid[k], 0.0), high
    centre, left, right = message(204), message(205), message(206)
    for n in (0, 2):
        m = n // 2
        wind[n, 0:8], wind[n, 136:144] = left[m], right[m]
        wind[n, 8:136] = jnp.concatenate([centre[m]] * 16, 0).T
        level_zero(n)

    def level(k, carry):
        v = lat_weights(wide[16, k, 8:16], wide[16, k, 0:8], wide[16, k, 16:24], sub)
        for m in range(13):
            latw[k, m] = v[m]
        for t in range(16):
            q = v[0] * wide[t, k, 2:10]
            for m in range(1, 13):
                q = q + v[m] * wide[t, k, 2 + m : 10 + m]
            swept[t, pl.ds(pl.multiple_of(8 * k, 8), 8), :] = q
        return carry

    lax.fori_loop(0, 16, level, 0)
    top[...] = latw[0]
    for t in range(16):
        out[t] = jnp.dot(matrix, swept[t], precision=hi, preferred_element_type=F32)


def emit_kernel(got, mixed_hbm, lonw, latw, column, out_hbm, grid, second, turned, wide, mixed, out, sems):
    copies = load([(mixed_hbm, mixed)], sems)
    sub = iota((8, 128), 0)
    spots = got[pl.ds(9, 128, stride=ROWS), :].T.astype(jnp.int32)
    row_of, col_of = spots >> 7, spots & 127

    def split(b):
        x = got[pl.ds(b, 128, stride=ROWS), :].T
        high = x.astype(BF16).astype(F32)
        return high, x - high

    def main(b):
        high, low = split(b)
        turned[0], turned[1] = high, low
        highs, lows, where = [], [], []
        target = iota((128, 128), 0)
        for s in range(8):
            here = row_of[8 * b + s : 8 * b + s + 1, :] == sub

            def rows(n):
                return jnp.concatenate(
                    [
                        jnp.where(here, jnp.broadcast_to(turned[n, 16 * s + t : 16 * s + t + 1, :], (8, 128)), 0.0)
                        for t in range(16)
                    ],
                    0,
                ).astype(BF16)

            highs.append(rows(0))
            lows.append(rows(1))
            where.append(jnp.where(col_of[8 * b + s : 8 * b + s + 1, :] == target, 1.0, 0.0).astype(BF16))
        where = jnp.concatenate(where, 1)
        return lax.dot_general(where, jnp.concatenate(highs, 1), NT, preferred_element_type=F32) + lax.dot_general(
            where, jnp.concatenate(lows, 1), NT, preferred_element_type=F32
        )

    expand = jnp.where((iota((32, 128), 0) & 15) == (iota((32, 128), 1) >> 3), 1.0, 0.0)
    diagonal = (iota((64, 128), 0) & 7) == (iota((64, 128), 1) & 7)

    def side(b, first):
        high, low = split(b)
        flux = jnp.concatenate(
            [jnp.concatenate([high[16 * s : 16 * s + 16], low[16 * s : 16 * s + 16]], 0) for s in range(8)], 1
        ).astype(BF16)
        key = (col_of - first) * 8 + row_of
        target = iota((64, 128), 0)
        where = jnp.concatenate(
            [jnp.where(key[8 * b + s : 8 * b + s + 1, :] == target, 1.0, 0.0) for s in range(8)], 1
        ).astype(BF16)
        sums = lax.dot_general(where, flux, NT, preferred_element_type=F32)
        sums = jnp.dot(sums, expand, precision=lax.Precision.HIGHEST, preferred_element_type=F32)
        sums = jnp.where(diagonal, sums, 0.0)
        return jnp.concatenate([jnp.sum(sums[8 * c : 8 * c + 8], 0, keepdims=True) for c in range(8)], 0)

    for n in range(3):
        grid[n, 0:8] = side(3 * n, 120)
        grid[n, 8:136] = main(3 * n + 1)
        grid[n, 136:144] = side(3 * n + 2, 0)
    for n in range(3):
        zonal_steps_unrolled(lonw.at[n], grid.at[n], second.at[n])
    for n in range(3):
        back = grid[n, 8:136].T
        for t in range(16):
            wide[t, 8 * n : 8 * n + 8] = back[8 * t : 8 * t + 8]

    copies[0].wait()

    def tracer(t):
        e = latw[0] * wide[t, 2:10]
        for m in range(1, 13):
            e = e + latw[m] * wide[t, 2 + m : 10 + m]
        for k in range(16):
            out[t, 8 * k : 8 * k + 8] = mixed[t, 8 * k : 8 * k + 8, :] + column[8 * k : 8 * k + 8, :] * e

    stores = []
    for n in range(4):
        for t in range(4 * n, 4 * n + 4):
            tracer(t)
        part = pl.ds(4 * n, 4)
        stores.append(pltpu.make_async_copy(out.at[part], out_hbm.at[part], sems.at[1 + n]))
        stores[-1].start()
    for c in stores:
        c.wait()


def call(kernel, ins, outs, scratch=(), kinds=None, copies=0, out_spec=None):
    spec = {"s": pltpu.SMEM, "v": VM, "h": pltpu.HBM}
    rooms = [VM(x, F32) if isinstance(x, tuple) else x for x in scratch]
    if copies:
        rooms.append(pltpu.SemaphoreType.DMA((copies,)))
    return pl.pallas_call(
        kernel,
        out_shape=[jax.ShapeDtypeStruct(s, F32) for s in outs],
        in_specs=[pl.BlockSpec(memory_space=spec[x]) for x in kinds],
        out_specs=[out_spec or vspec()] * len(outs),
        scratch_shapes=rooms,
        compiler_params=PARAMS,
    )(*[pltpu.with_memory_space_constraint(x, pltpu.HBM) if k == "h" else x for x, k in zip(ins, kinds)])


def load(pairs, sems):
    copies = [pltpu.make_async_copy(x, y, sems.at[n]) for n, (x, y) in enumerate(pairs)]
    for c in copies:
        c.start()
    return copies


def on_device(
    features, land_tile, land_spot, w_in, b_in, w_mid, b_mid, w_out, tracers, zonal_wind, meridional_wind, mixing
):
    ids = jnp.stack([lax.axis_index("lat"), lax.axis_index("lon")]).astype(jnp.int32)
    shape = tracers.shape
    tracers = tracers.reshape(16, 128, 128)
    zonal = zonal_wind.reshape(128, 128)
    pack_a, pack_b, turned = call(
        pack_kernel,
        (ids, tracers, zonal),
        [(17, 8, 128), (17, 8, 128), (17, 128, 128)],
        scratch=[(16, 128, 128), (128, 128)],
        kinds="shh",
        copies=5,
    )
    lon_a = [(i, i ^ 1) for i in range(16)]
    lon_b = [(i, (i + 1) % 16 if i & 1 else (i - 1) % 16) for i in range(16)]
    lat_a = [(i, i ^ 1) for i in range(8)]
    lat_b = [(i, i + 1 if i & 1 else i - 1) for i in range(1, 7)]
    halo_b = lax.ppermute(pack_b, "lon", lon_b)
    halo_a = lax.ppermute(pack_a, "lon", lon_a)
    cells = features.shape[0]
    inputs = (
        features.T,
        land_tile.reshape(1, cells),
        land_spot.reshape(1, cells),
        w_in,
        b_in.reshape(1, -1),
        w_mid,
        b_mid.reshape(1, -1),
        w_out.T,
    )
    (message,) = call(
        flux_kernel,
        inputs,
        [(128 * ROWS, 128)],
        scratch=[VM(x.shape, x.dtype) for x in inputs],
        kinds="h" * 8,
        copies=8,
    )
    halo_a, halo_b, message = lax.optimization_barrier((halo_a, halo_b, message))
    state, row_a, row_b, edge = call(
        lon_kernel,
        (ids, turned, zonal, meridional_wind, halo_a, halo_b),
        [(16, 128, 128), (LATMSG, 8, 128), (LATMSG, 8, 128), (144, 128)],
        scratch=[(7, 136, 128), (16, 144, 128), (16, 136, 128), (16, 8, 128), (8, 128)],
        kinds="svhhvv",
        copies=2,
    )
    rows_a = lax.ppermute(row_a, "lat", lat_a)
    rows_b = lax.ppermute(row_b, "lat", lat_b)
    got = lax.all_to_all(
        message.reshape(128, 1, ROWS * 128), ("lat", "lon"), split_axis=0, concat_axis=0, tiled=True
    ).reshape(128 * ROWS, 128)
    mixed, lonw, latw, column = call(
        lat_kernel,
        (ids, state, meridional_wind, rows_a, rows_b, edge, mixing.reshape(128, 16)),
        [(16, 128, 128), (3, 7, 136, 128), (13, 8, 128), (128, 128)],
        scratch=[
            (16, 128, 128),
            (17, 16, 24, 128),
            (3, 144, 128),
            (16, 13, 8, 128),
            (16, 8, 128),
            (LATMSG, 8, 128),
            (LATMSG, 8, 128),
            (128, 16),
        ],
        kinds="svhhhvh",
        copies=4,
    )
    (out,) = call(
        emit_kernel,
        (got, mixed, lonw, latw, column),
        [(16, 128, 128)],
        scratch=[(3, 144, 128), (3, 136, 128), (2, 128, 128), (16, 24, 128), (16, 128, 128), (16, 128, 128)],
        kinds="vhvvv",
        copies=5,
        out_spec=pl.BlockSpec(memory_space=pl.ANY),
    )
    return out.reshape(shape)


def solution(mesh):
    placed = (
        P(("lat", "lon"), None),
        P(("lat", "lon"), None),
        P(("lat", "lon")),
        P(),
        P(),
        P(),
        P(),
        P(),
        P(None, None, "lat", "lon"),
        P(None, "lat", "lon"),
        P(None, "lat", "lon"),
        P("lat", None, None),
    )
    return jax.shard_map(
        on_device,
        mesh=mesh,
        in_specs=placed,
        out_specs=P(None, None, "lat", "lon"),
        check_vma=False,
    )
```

time: 80.6 us -> 61.2 us (0.76)
  the two profiles are of different devices: /device:TPU:31 before, /device:TPU:1 now
where the time goes in v2:
time: 61.2 us; the launch traced here: 61 us
  waiting for transfers between devices  21.1 us (34%)
  Pallas kernels  19.6 us (32%)
  starting transfers between devices  19.1 us (31%)
  local copies, waits for them, and re-layouts  0.99 us (2%)
    pallas_call x5, Pallas kernels, call(): pl.pallas_call(kernel, out_shape=[jax.ShapeDtypeStruct(s, F32) for s in o...  19.6 us
    all_to_all x1, waiting for transfers between devices, on_device(): lax.all_to_all(message.reshape(128, 1, ROWS * 128), ('lat', 'lon'), split...  17.5 us
    all_to_all x1, starting transfers between devices, on_device(): lax.all_to_all(message.reshape(128, 1, ROWS * 128), ('lat', 'lon'), split...  11.5 us
    ppermute x1, waiting for transfers between devices, on_device(): rows_a = lax.ppermute(row_a, 'lat', lat_a)  3.56 us
    ppermute x1, starting transfers between devices, on_device(): halo_b = lax.ppermute(pack_b, 'lon', lon_b)  2.8 us
    ppermute x1, starting transfers between devices, on_device(): rows_a = lax.ppermute(row_a, 'lat', lat_a)  1.71 us
    ppermute x1, starting transfers between devices, on_device(): rows_b = lax.ppermute(row_b, 'lat', lat_b)  1.55 us
    ppermute x1, starting transfers between devices, on_device(): halo_a = lax.ppermute(pack_a, 'lon', lon_a)  1.5 us
  transfers between devices with their start and end apart: 5, of which 2 were waited for; matrix products, arithmetic and copies ran while one was open for 0% of the time, Pallas kernels for 16%

profile of v2, /device:TPU:1, one launch (start us, length us, event | category | flops | bytes accessed | tf_op | source)
XLA Modules:
  0.0 61.0 jit_solution(16571464910508457572)
XLA Ops:
  0.0 0.1 pad_add_fusion.ids
  0.1 2.1 %shard_map.118 = (f32[17,8,128]{2,1,0:T(8,128)S(1)}, f32[17,8,128]{2,1,0:T(8,128)S(1)}, f32[17,128,128]{2,1,0:T(8,128)S(1)}) custom-call(s32[2]{0:T(128)S(1)} %pad_add_fusion.ids, f32[16,128,128]{2,1,0:T(8,128)} %bitcast.15, f32[128,128]{1,0:T(8,128)} %bitcast.16), custom_call_target="tpu_custom_call" | custom-call | tf_op jit(solution)/shard_map/pallas_call | solution.py:458
  2.2 1.5 %collective-permute-start = (f32[17,8,128]{2,1,0:T(8,128)S(1)}, f32[17,8,128]{2,1,0:T(8,128)S(1)}, u32[]{:S(2)}, u32[]{:S(2)}) collective-permute-start(f32[17,8,128]{2,1,0:T(8,128)S(1)} %get-tuple-element.19), channel_id=1, source_target_pairs={{0,1},{1,0},{2,3},{3,2},{4,5},{5,4},{6,7},{7,6},{8,9},{9,8},{10,11... | collective-permute-start | bytes 208904 | tf_op jit(solution)/shard_map/ppermute | solution.py:495
  3.7 2.8 %collective-permute-start.1 = (f32[17,8,128]{2,1,0:T(8,128)S(1)}, f32[17,8,128]{2,1,0:T(8,128)S(1)}, u32[]{:S(2)}, u32[]{:S(2)}) collective-permute-start(f32[17,8,128]{2,1,0:T(8,128)S(1)} %get-tuple-element.20), channel_id=1, source_target_pairs={{0,15},{1,2},{2,1},{3,4},{4,3},{5,6},{6,5},{7,8},{8,7},{9,10},{10,... | collective-permute-start | bytes 208904 | tf_op jit(solution)/shard_map/ppermute | solution.py:494
  6.5 2.9 %shard_map.119 = f32[1280,128]{1,0:T(8,128)} custom-call(bf16[64,512]{1,0:T(8,128)(2,1)} %bitcast.18, s32[1,512]{1,0:T(1,128)} %bitcast.21, s32[1,512]{1,0:T(1,128)} %bitcast.22, bf16[64,256]{1,0:T(8,128)(2,1)} %refs_3_.1, f32[1,256]{1,0:T(1,128)} %bitcast.23, bf16[256,256]{1,0:T(8,128)(2,1)} %refs_5_.1, f32[1,256]{1,0:T(1,128)} %bitcast.24, ...), custom_call_target="tpu_custom_call" | custom-call | tf_op jit(solution)/shard_map/pallas_call | solution.py:458
  9.4 0.0 collective-permute-done.halo_a
  9.5 0.0 collective-permute-done.1.halo_b
  9.5 3.7 %shard_map.120 = (f32[16,128,128]{2,1,0:T(8,128)S(1)}, f32[207,8,128]{2,1,0:T(8,128)}, f32[207,8,128]{2,1,0:T(8,128)S(1)}, f32[144,128]{1,0:T(8,128)S(1)}) custom-call(s32[2]{0:T(128)S(1)} %pad_add_fusion.ids, f32[17,128,128]{2,1,0:T(8,128)S(1)} %get-tuple-element.22.turned, f32[128,128]{1,0:T(8,128)} %bitcast.17, f32[16,8,128]{2,1,0:T(8,128)} %merid_hbm.3, ...), custom_call_target="tpu_custom_call" | custom-call | tf_op jit(solution)/shard_map/pallas_call | solution.py:458
  13.1 1.7 %collective-permute-start.2 = (f32[207,8,128]{2,1,0:T(8,128)}, f32[207,8,128]{2,1,0:T(8,128)}, u32[]{:S(2)}, u32[]{:S(2)}) collective-permute-start(f32[207,8,128]{2,1,0:T(8,128)} %get-tuple-element.26), channel_id=1, source_target_pairs={{0,16},{16,0},{32,48},{48,32},{64,80},{80,64},{96,112},{112,96},{1... | collective-permute-start | bytes 2543624 | tf_op jit(solution)/shard_map/ppermute | solution.py:524
  14.9 1.6 %collective-permute-start.3 = (f32[207,8,128]{2,1,0:T(8,128)S(1)}, f32[207,8,128]{2,1,0:T(8,128)}, u32[]{:S(2)}, u32[]{:S(2)}) collective-permute-start(f32[207,8,128]{2,1,0:T(8,128)S(1)} %get-tuple-element.27), channel_id=1, source_target_pairs={{16,32},{32,16},{48,64},{64,48},{80,96},{96,80},{17,33},{33,17},{4... | collective-permute-start | bytes 2543624 | tf_op jit(solution)/shard_map/ppermute | solution.py:525
  16.4 11.5 %all-to-all-start = ((f32[128,1,1280]{2,1,0:T(1,128)}), f32[128,1,1280]{2,1,0:T(1,128)S(1)}, u32[]{:S(2)}, u32[]{:S(2)}) async-start(f32[128,1,1280]{2,1,0:T(1,128)} %bitcast.10), calls=%async_computation | async-start | bytes 1310720 | tf_op jit(solution)/shard_map/all_to_all | solution.py:526
  27.9 3.6 %collective-permute-done.2.a_hbm = f32[207,8,128]{2,1,0:T(8,128)} collective-permute-done((f32[207,8,128]{2,1,0:T(8,128)}, f32[207,8,128]{2,1,0:T(8,128)}, u32[]{:S(2)}, u32[]{:S(2)}) %collective-permute-start.2) | collective-permute-done | bytes 847904 | tf_op jit(solution)/shard_map/ppermute | solution.py:524
  31.5 0.0 collective-permute-done.3.b_hbm
  31.5 6.9 %shard_map.121 = (f32[16,128,128]{2,1,0:T(8,128)S(1)}, f32[3,7,136,128]{3,2,1,0:T(8,128)S(1)}, f32[13,8,128]{2,1,0:T(8,128)S(1)}, f32[128,128]{1,0:T(8,128)S(1)}) custom-call(s32[2]{0:T(128)S(1)} %pad_add_fusion.ids, f32[16,128,128]{2,1,0:T(8,128)S(1)} %get-tuple-element.25.state, f32[16,8,128]{2,1,0:T(8,128)} %merid_hbm.3, ...), custom_call_target="tpu_custom_call" | custom-call | tf_op jit(solution)/shard_map/pallas_call | solution.py:458
  38.4 0.0 copy-start
  38.4 1.0 %copy-done = f32[16,128,128]{2,1,0:T(8,128)} copy-done((f32[16,128,128]{2,1,0:T(8,128)}, f32[16,128,128]{2,1,0:T(8,128)S(1)}, u32[]{:S(2)}) %copy-start) | copy-done | bytes 1048600
  39.4 17.5 %all-to-all-done = f32[128,1,1280]{2,1,0:T(1,128)S(1)} async-done(((f32[128,1,1280]{2,1,0:T(1,128)}), f32[128,1,1280]{2,1,0:T(1,128)S(1)}, u32[]{:S(2)}, u32[]{:S(2)}) %all-to-all-start) | async-done | bytes 655392 | tf_op jit(solution)/shard_map/all_to_all | solution.py:526
  57.0 4.0 %shard_map.122 = f32[16,128,128]{2,1,0:T(8,128)} custom-call(f32[1280,128]{1,0:T(8,128)S(1)} %bitcast.14, f32[16,128,128]{2,1,0:T(8,128)} %copy-done, f32[3,7,136,128]{3,2,1,0:T(8,128)S(1)} %get-tuple-element.30.lonw, f32[13,8,128]{2,1,0:T(8,128)S(1)} %get-tuple-element.31.latw, f32[128,128]{1,0:T(8,128)S(1)} %get-tuple-element.32.column), custom_call_target="tpu_custom_call" | custom-call | tf_op jit(solution)/shard_map/pallas_call | solution.py:458
Async XLA Ops:
  2.2 7.2 %collective-permute-start = (f32[17,8,128]{2,1,0:T(8,128)S(1)}, f32[17,8,128]{2,1,0:T(8,128)S(1)}, u32[]{:S(2)}, u32[]{:S(2)}) collective-permute-start(f32[17,8,128]{2,1,0:T(8,128)S(1)} %get-tuple-element.19), channel_id=1, source_target_pairs={{0,1},{1,0},{2,3},{3,2},{4,5},{5,4},{6,7},{7,6},{8,9},{9,8},{10,11... | collective-permute-start | bytes 208904 | tf_op jit(solution)/shard_map/ppermute | solution.py:495
  3.7 5.8 %collective-permute-start.1 = (f32[17,8,128]{2,1,0:T(8,128)S(1)}, f32[17,8,128]{2,1,0:T(8,128)S(1)}, u32[]{:S(2)}, u32[]{:S(2)}) collective-permute-start(f32[17,8,128]{2,1,0:T(8,128)S(1)} %get-tuple-element.20), channel_id=1, source_target_pairs={{0,15},{1,2},{2,1},{3,4},{4,3},{5,6},{6,5},{7,8},{8,7},{9,10},{10,... | collective-permute-start | bytes 208904 | tf_op jit(solution)/shard_map/ppermute | solution.py:494
  13.1 18.3 %collective-permute-start.2 = (f32[207,8,128]{2,1,0:T(8,128)}, f32[207,8,128]{2,1,0:T(8,128)}, u32[]{:S(2)}, u32[]{:S(2)}) collective-permute-start(f32[207,8,128]{2,1,0:T(8,128)} %get-tuple-element.26), channel_id=1, source_target_pairs={{0,16},{16,0},{32,48},{48,32},{64,80},{80,64},{96,112},{112,96},{1... | collective-permute-start | bytes 2543624 | tf_op jit(solution)/shard_map/ppermute | solution.py:524
  14.9 16.6 %collective-permute-start.3 = (f32[207,8,128]{2,1,0:T(8,128)S(1)}, f32[207,8,128]{2,1,0:T(8,128)}, u32[]{:S(2)}, u32[]{:S(2)}) collective-permute-start(f32[207,8,128]{2,1,0:T(8,128)S(1)} %get-tuple-element.27), channel_id=1, source_target_pairs={{16,32},{32,16},{48,64},{64,48},{80,96},{96,80},{17,33},{33,17},{4... | collective-permute-start | bytes 2543624 | tf_op jit(solution)/shard_map/ppermute | solution.py:525
  16.4 40.6 %all-to-all-start = ((f32[128,1,1280]{2,1,0:T(1,128)}), f32[128,1,1280]{2,1,0:T(1,128)S(1)}, u32[]{:S(2)}, u32[]{:S(2)}) async-start(f32[128,1,1280]{2,1,0:T(1,128)} %bitcast.10), calls=%async_computation | async-start | bytes 1310720 | tf_op jit(solution)/shard_map/all_to_all | solution.py:526
  38.4 1.0 %copy-start = (f32[16,128,128]{2,1,0:T(8,128)}, f32[16,128,128]{2,1,0:T(8,128)S(1)}, u32[]{:S(2)}) copy-start(f32[16,128,128]{2,1,0:T(8,128)S(1)} %get-tuple-element.29.mixed_hbm) | copy-start | bytes 3145732

commit v3 on v2

--- a/solution.py
+++ b/solution.py
@@ -10,7 +10,11 @@
 NT = (((1,), (1,)), ((), ()))
 TN = (((0,), (0,)), ((), ()))
 ROWS = 10
-LATMSG = 17 * 12 + 3
+N1 = 8
+N2 = 16 - N1
+WIND = 12 * N1
+MSG1 = WIND + 15
+MSG2 = 12 * N2
 VM = pltpu.VMEM
 PARAMS = pltpu.CompilerParams(vmem_limit_bytes=12 * 1024 * 1024)
 
@@ -81,14 +85,11 @@
 
 
 def zonal_weights(wind, out):
-    def block(b, carry):
-        f = face_weights(wind[pl.ds(8 * b + 5, 8), :])
-        before = face_weights(wind[pl.ds(8 * b + 4, 8), :])
+    for b in range(17):
+        f = face_weights(wind[8 * b + 5 : 8 * b + 13])
+        before = face_weights(wind[8 * b + 4 : 8 * b + 12])
         for m, w in enumerate(step_weights(f, before)):
-            out[m, pl.ds(pl.multiple_of(8 * b, 8), 8), :] = w
-        return carry
-
-    lax.fori_loop(0, 17, block, 0)
+            out[m, 8 * b : 8 * b + 8] = w
 
 
 def zonal_steps_unrolled(weights, first, second):
@@ -225,100 +226,167 @@
     out[pl.ds(9, 128, stride=ROWS), :] = places_out
 
 
-def lon_kernel(
-    ids, turned, zonal, merid_hbm, halo_a, halo_b, state, out_a, out_b, wind, weights, first, second, merid, surface, sems
-):
-    copies = load([(merid_hbm, merid), (zonal.at[pl.ds(0, 8)], surface)], sems)
+def sweep_columns(ids, base, count, turned, halo_a, halo_b, state, weights, first, second):
     odd = (ids[1] & 1) == 1
+    for t in range(count):
+        a, b = halo_a[base + t], halo_b[base + t]
+        first[t, 0:8], first[t, 136:144] = jnp.where(odd, a, b), jnp.where(odd, b, a)
+        first[t, 8:136] = turned[base + t]
+    zonal_steps(weights, first, second, count)
+    for t in range(count):
+        state[t] = first[t, 8:136].T
+
+
+def row_packer(ids, out_a, out_b):
     odd_lat = (ids[0] & 1) == 1
     sub = iota((8, 128), 0)
-
-    def halo(t):
-        a, b = halo_a[t], halo_b[t]
-        return jnp.where(odd, a, b), jnp.where(odd, b, a)
-
-    left, right = halo(16)
-    wind[0:8], wind[8:136], wind[136:144] = left, turned[16], right
-    zonal_weights(wind, weights)
-    for t in range(16):
-        low, high = halo(t)
-        first[t, 0:8], first[t, 8:136], first[t, 136:144] = low, turned[t], high
-    zonal_steps(weights, first, second, 16)
-    for t in range(16):
-        state[t] = first[t, 8:136].T
 
     def emit(n, up, down):
         out_a[n] = jnp.where(odd_lat, down, up)
         out_b[n] = jnp.where(odd_lat, up, down)
 
-    def pack(t, read):
+    def pack(n, read):
         for g in range(4):
             q = [read(4 * g + i) for i in range(4)]
             for i in range(3):
                 last = pltpu.roll(q[3], 6 - 2 * i, 0)
-                emit(t * 12 + g * 3 + i, jnp.where(sub >= 2, q[i], last), jnp.where(sub < 6, q[i], last))
+                emit(n + g * 3 + i, jnp.where(sub >= 2, q[i], last), jnp.where(sub < 6, q[i], last))
+
+    return emit, pack
+
+
+def lon_first_kernel(
+    ids, turned, zonal, merid_hbm, halo_a, halo_b, state_hbm, out_a, out_b, wind, weights, first, second, merid, surface, state, sems
+):
+    copies = load([(merid_hbm, merid), (zonal.at[pl.ds(0, 8)], surface)], sems)
+    odd = (ids[1] & 1) == 1
+    a, b = halo_a[16], halo_b[16]
+    left, right = jnp.where(odd, a, b), jnp.where(odd, b, a)
+    wind[0:8], wind[8:136], wind[136:144] = left, turned[16], right
+    zonal_weights(wind, weights)
+    sweep_columns(ids, 0, N1, turned, halo_a, halo_b, state, weights, first, second)
+    store = pltpu.make_async_copy(state, state_hbm, sems.at[2])
+    store.start()
+    emit, pack = row_packer(ids, out_a, out_b)
 
     def body(t, carry):
-        pack(t, lambda k: state[t, 8 * k : 8 * k + 8, :])
+        pack(12 * t, lambda k: state[t, 8 * k : 8 * k + 8, :])
         return carry
 
-    lax.fori_loop(0, 16, body, 0)
-    keep = jnp.logical_or(sub < 7, ids[0] < 7)
+    lax.fori_loop(0, N1, body, 0)
+    keep = jnp.logical_or(iota((8, 128), 0) < 7, ids[0] < 7)
     for c in copies:
         c.wait()
-    pack(16, lambda k: jnp.where(keep, merid[k], 0.0))
-    emit(204, surface[...], surface[...])
-    emit(205, left, left)
-    emit(206, right, right)
-
-
-def lat_kernel(
+    pack(WIND, lambda k: jnp.where(keep, merid[k], 0.0))
+    emit(WIND + 12, surface[...], surface[...])
+    emit(WIND + 13, left, left)
+    emit(WIND + 14, right, right)
+    store.wait()
+
+
+def lon_second_kernel(ids, turned, halo_a, halo_b, weights, state_hbm, out_a, out_b, first, second, state, sems):
+    sweep_columns(ids, N1, N2, turned, halo_a, halo_b, state, weights, first, second)
+    store = pltpu.make_async_copy(state, state_hbm, sems.at[0])
+    store.start()
+    _, pack = row_packer(ids, out_a, out_b)
+
+    def body(t, carry):
+        pack(12 * t, lambda k: state[t, 8 * k : 8 * k + 8, :])
+        return carry
+
+    lax.fori_loop(0, N2, body, 0)
+    store.wait()
+
+
+def row_reader(ids, halo_a, halo_b):
+    odd_lat = (ids[0] & 1) == 1
+    sub = iota((8, 128), 0)
+
+    def message(n):
+        a, b = halo_a[n], halo_b[n]
+        return jnp.where(odd_lat, a, b), jnp.where(odd_lat, b, a)
+
+    def four(n):
+        got = [message(n + x) for x in range(3)]
+        rolled = [[pltpu.roll(got[x][y], 2 + 2 * x, 0) for x in range(3)] for y in range(2)]
+        low = jnp.where(sub < 4, rolled[0][0], jnp.where(sub < 6, rolled[0][1], rolled[0][2]))
+        high = jnp.where(sub < 2, rolled[1][0], jnp.where(sub < 4, rolled[1][1], rolled[1][2]))
+        return got + [(low, high)]
+
+    return message, four
+
+
+def sweep_rows(count, four, latw, wide, swept):
+    def unpack(t, carry):
+        for g in range(4):
+            for x, (low, high) in enumerate(four(12 * t + 3 * g)):
+                k = 4 * g + x
+                wide[t, k, 0:8], wide[t, k, 16:24] = low, high
+        return carry
+
+    lax.fori_loop(0, count, unpack, 0, unroll=2)
+
+    def level(k, carry):
+        v = [latw[k, m] for m in range(13)]
+        for t in range(count):
+            q = v[0] * wide[t, k, 2:10]
+            for m in range(1, 13):
+                q = q + v[m] * wide[t, k, 2 + m : 10 + m]
+            swept[t, pl.ds(pl.multiple_of(8 * k, 8), 8), :] = q
+        return carry
+
+    lax.fori_loop(0, 16, level, 0)
+
+
+def mix(matrix, x):
+    high = x.astype(BF16)
+    low = (x - high.astype(F32)).astype(BF16)
+    return (
+        jnp.dot(matrix[0], high, preferred_element_type=F32)
+        + jnp.dot(matrix[0], low, preferred_element_type=F32)
+        + jnp.dot(matrix[1], high, preferred_element_type=F32)
+    )
+
+
+def parts(x):
+    high = x.astype(BF16)
+    return high, (x - high.astype(F32)).astype(BF16)
+
+
+def rows_kernel(
     ids,
-    state,
+    state_hbm,
     merid_hbm,
     a_hbm,
     b_hbm,
     edge,
     mixing_hbm,
-    out,
-    lonw,
-    top,
-    column,
+    grid_in,
+    out_hbm,
+    latw,
+    matrix,
+    emitted,
     swept,
     wide,
     wind,
-    latw,
     merid,
     halo_a,
     halo_b,
     mixing,
+    lonw,
+    grid,
+    second,
+    back,
+    out,
     sems,
 ):
-    copies = load([(a_hbm, halo_a), (b_hbm, halo_b), (merid_hbm, merid), (mixing_hbm, mixing)], sems)
-    odd_lat = (ids[0] & 1) == 1
+    copies = load(
+        [(a_hbm, halo_a), (b_hbm, halo_b), (merid_hbm, merid), (mixing_hbm, mixing), (state_hbm, wide.at[:, :, pl.ds(8, 8), :])], sems
+    )
     sub = iota((8, 128), 0)
     keep = jnp.logical_or(sub < 7, ids[0] < 7)
     hi = lax.Precision.HIGHEST
     i, j = iota((128, 128), 0), iota((128, 128), 1)
-
-    def message(n):
-        a, b = halo_a[n], halo_b[n]
-        return jnp.where(odd_lat, a, b), jnp.where(odd_lat, b, a)
-
-    def four(t, g):
-        got = [message(t * 12 + g * 3 + x) for x in range(3)]
-        rolled = [[pltpu.roll(got[x][y], 2 + 2 * x, 0) for x in range(3)] for y in range(2)]
-        low = jnp.where(sub < 4, rolled[0][0], jnp.where(sub < 6, rolled[0][1], rolled[0][2]))
-        high = jnp.where(sub < 2, rolled[1][0], jnp.where(sub < 4, rolled[1][1], rolled[1][2]))
-        return got + [(low, high)]
-
-    def unpack(t, carry):
-        for g in range(4):
-            for x, (low, high) in enumerate(four(t, g)):
-                k = 4 * g + x
-                wide[t, k, 0:8], wide[t, k, 8:16], wide[t, k, 16:24] = low, state[t, 8 * k : 8 * k + 8, :], high
-        return carry
-
     spread = jnp.where((j & 7) == i, 1.0, 0.0)
 
     def level_zero(n):
@@ -331,42 +399,67 @@
     order = jnp.where(((i & 7) * 16 + (i >> 3)) == j, 1.0, 0.0)
     by_level = jnp.dot(order, mixing[...], precision=hi, preferred_element_type=F32)
     expand = jnp.where((iota((16, 128), 1) >> 3) == iota((16, 128), 0), 1.0, 0.0)
-    matrix = jnp.dot(by_level, expand, precision=hi, preferred_element_type=F32)
-    matrix = jnp.where((i & 7) == (j & 7), matrix, 0.0)
-    column[...] = jnp.broadcast_to(by_level[:, 0:1], (128, 128))
-    for c in copies[:3]:
+    whole = jnp.dot(by_level, expand, precision=hi, preferred_element_type=F32)
+    whole = jnp.where((i & 7) == (j & 7), whole, 0.0)
+    matrix[...] = whole
+    for c in copies[:3] + copies[4:]:
         c.wait()
-    lax.fori_loop(0, 16, unpack, 0)
+    message, four = row_reader(ids, halo_a, halo_b)
     for g in range(4):
-        for x, (low, high) in enumerate(four(16, g)):
+        for x, (low, high) in enumerate(four(WIND + 3 * g)):
             k = 4 * g + x
-            wide[16, k, 0:8], wide[16, k, 8:16], wide[16, k, 16:24] = low, jnp.where(keep, merid[k], 0.0), high
-    centre, left, right = message(204), message(205), message(206)
+            v = lat_weights(jnp.where(keep, merid[k], 0.0), low, high, sub)
+            for m in range(13):
+                latw[k, m] = v[m]
+    centre, left, right = message(WIND + 12), message(WIND + 13), message(WIND + 14)
     for n in (0, 2):
         m = n // 2
         wind[n, 0:8], wind[n, 136:144] = left[m], right[m]
         wind[n, 8:136] = jnp.concatenate([centre[m]] * 16, 0).T
         level_zero(n)
-
-    def level(k, carry):
-        v = lat_weights(wide[16, k, 8:16], wide[16, k, 0:8], wide[16, k, 16:24], sub)
-        for m in range(13):
-            latw[k, m] = v[m]
+    for n in range(3):
+        grid[n] = grid_in[n]
+        zonal_steps_unrolled(lonw.at[n], grid.at[n], second.at[n])
+    for n in range(3):
+        x = grid[n, 8:136].T
         for t in range(16):
-            q = v[0] * wide[t, k, 2:10]
-            for m in range(1, 13):
-                q = q + v[m] * wide[t, k, 2 + m : 10 + m]
-            swept[t, pl.ds(pl.multiple_of(8 * k, 8), 8), :] = q
-        return carry
-
-    lax.fori_loop(0, 16, level, 0)
-    top[...] = latw[0]
+            back[t, 8 * n : 8 * n + 8] = x[8 * t : 8 * t + 8]
     for t in range(16):
-        out[t] = jnp.dot(matrix, swept[t], precision=hi, preferred_element_type=F32)
-
-
-def emit_kernel(got, mixed_hbm, lonw, latw, column, out_hbm, grid, second, turned, wide, mixed, out, sems):
-    copies = load([(mixed_hbm, mixed)], sems)
+        e = latw[0, 0] * back[t, 2:10]
+        for m in range(1, 13):
+            e = e + latw[0, m] * back[t, 2 + m : 10 + m]
+        emitted[t] = e
+    sweep_rows(N1, four, latw, wide, swept)
+    split = parts(whole)
+    for t in range(N1):
+        swept[t, 0:8] = swept[t, 0:8] + emitted[t]
+        out[t] = mix(split, swept[t])
+    store = pltpu.make_async_copy(out, out_hbm.at[pl.ds(0, N1)], sems.at[0])
+    store.start()
+    store.wait()
+
+
+def last_kernel(ids, state_hbm, halo_a, halo_b, latw, matrix, emitted, _, out_hbm, swept, wide, out, sems):
+    copies = load([(state_hbm, wide.at[:, :, pl.ds(8, 8), :])], sems)
+    split = parts(matrix[...])
+    copies[0].wait()
+    _, four = row_reader(ids, halo_a, halo_b)
+    sweep_rows(N2, four, latw, wide, swept)
+    half = N2 // 2
+    stores = []
+    for n, (first, count) in enumerate(((0, half), (half, N2 - half))):
+        for t in range(first, first + count):
+            swept[t, 0:8] = swept[t, 0:8] + emitted[N1 + t]
+            out[t] = mix(split, swept[t])
+        stores.append(
+            pltpu.make_async_copy(out.at[pl.ds(first, count)], out_hbm.at[pl.ds(N1 + first, count)], sems.at[1 + n])
+        )
+        stores[-1].start()
+    for c in stores:
+        c.wait()
+
+
+def scatter_kernel(got, grid, turned):
     sub = iota((8, 128), 0)
     spots = got[pl.ds(9, 128, stride=ROWS), :].T.astype(jnp.int32)
     row_of, col_of = spots >> 7, spots & 127
@@ -423,45 +516,22 @@
         grid[n, 0:8] = side(3 * n, 120)
         grid[n, 8:136] = main(3 * n + 1)
         grid[n, 136:144] = side(3 * n + 2, 0)
-    for n in range(3):
-        zonal_steps_unrolled(lonw.at[n], grid.at[n], second.at[n])
-    for n in range(3):
-        back = grid[n, 8:136].T
-        for t in range(16):
-            wide[t, 8 * n : 8 * n + 8] = back[8 * t : 8 * t + 8]
-
-    copies[0].wait()
-
-    def tracer(t):
-        e = latw[0] * wide[t, 2:10]
-        for m in range(1, 13):
-            e = e + latw[m] * wide[t, 2 + m : 10 + m]
-        for k in range(16):
-            out[t, 8 * k : 8 * k + 8] = mixed[t, 8 * k : 8 * k + 8, :] + column[8 * k : 8 * k + 8, :] * e
-
-    stores = []
-    for n in range(4):
-        for t in range(4 * n, 4 * n + 4):
-            tracer(t)
-        part = pl.ds(4 * n, 4)
-        stores.append(pltpu.make_async_copy(out.at[part], out_hbm.at[part], sems.at[1 + n]))
-        stores[-1].start()
-    for c in stores:
-        c.wait()
-
-
-def call(kernel, ins, outs, scratch=(), kinds=None, copies=0, out_spec=None):
+
+
+def call(kernel, ins, outs, scratch=(), kinds=None, copies=0, in_hbm=(), aliases=None, us=2):
     spec = {"s": pltpu.SMEM, "v": VM, "h": pltpu.HBM}
     rooms = [VM(x, F32) if isinstance(x, tuple) else x for x in scratch]
     if copies:
         rooms.append(pltpu.SemaphoreType.DMA((copies,)))
     return pl.pallas_call(
         kernel,
-        out_shape=[jax.ShapeDtypeStruct(s, F32) for s in outs],
+        out_shape=[pltpu.HBM(s, F32) if n in in_hbm else jax.ShapeDtypeStruct(s, F32) for n, s in enumerate(outs)],
         in_specs=[pl.BlockSpec(memory_space=spec[x]) for x in kinds],
-        out_specs=[out_spec or vspec()] * len(outs),
+        out_specs=[pl.BlockSpec(memory_space=pltpu.HBM if n in in_hbm else VM) for n in range(len(outs))],
         scratch_shapes=rooms,
         compiler_params=PARAMS,
+        cost_estimate=pl.CostEstimate(flops=0, bytes_accessed=int(us * 3.6e6), transcendentals=0),
+        input_output_aliases=aliases or {},
     )(*[pltpu.with_memory_space_constraint(x, pltpu.HBM) if k == "h" else x for x, k in zip(ins, kinds)])
 
 
@@ -484,6 +554,7 @@
         (ids, tracers, zonal),
         [(17, 8, 128), (17, 8, 128), (17, 128, 128)],
         scratch=[(16, 128, 128), (128, 128)],
+        us=2,
         kinds="shh",
         copies=5,
     )
@@ -509,48 +580,77 @@
         inputs,
         [(128 * ROWS, 128)],
         scratch=[VM(x.shape, x.dtype) for x in inputs],
+        us=3,
         kinds="h" * 8,
         copies=8,
     )
     halo_a, halo_b, message = lax.optimization_barrier((halo_a, halo_b, message))
-    state, row_a, row_b, edge = call(
-        lon_kernel,
+    state_one, one_a, one_b, edge, weights = call(
+        lon_first_kernel,
         (ids, turned, zonal, meridional_wind, halo_a, halo_b),
-        [(16, 128, 128), (LATMSG, 8, 128), (LATMSG, 8, 128), (144, 128)],
-        scratch=[(7, 136, 128), (16, 144, 128), (16, 136, 128), (16, 8, 128), (8, 128)],
+        [(N1, 128, 128), (MSG1, 8, 128), (MSG1, 8, 128), (144, 128), (7, 136, 128)],
+        scratch=[(N1, 144, 128), (N1, 136, 128), (16, 8, 128), (8, 128), (N1, 128, 128)],
+        us=3,
         kinds="svhhvv",
-        copies=2,
-    )
-    rows_a = lax.ppermute(row_a, "lat", lat_a)
-    rows_b = lax.ppermute(row_b, "lat", lat_b)
+        copies=3,
+        in_hbm=(0,),
+    )
+    ones_a = lax.ppermute(one_a, "lat", lat_a)
+    ones_b = lax.ppermute(one_b, "lat", lat_b)
     got = lax.all_to_all(
         message.reshape(128, 1, ROWS * 128), ("lat", "lon"), split_axis=0, concat_axis=0, tiled=True
     ).reshape(128 * ROWS, 128)
-    mixed, lonw, latw, column = call(
-        lat_kernel,
-        (ids, state, meridional_wind, rows_a, rows_b, edge, mixing.reshape(128, 16)),
-        [(16, 128, 128), (3, 7, 136, 128), (13, 8, 128), (128, 128)],
+    state_two, two_a, two_b = call(
+        lon_second_kernel,
+        (ids, turned, halo_a, halo_b, weights),
+        [(N2, 128, 128), (MSG2, 8, 128), (MSG2, 8, 128)],
+        scratch=[(N2, 144, 128), (N2, 136, 128), (N2, 128, 128)],
+        us=3,
+        kinds="svvvv",
+        copies=1,
+        in_hbm=(0,),
+    )
+    twos_a = lax.ppermute(two_a, "lat", lat_a)
+    twos_b = lax.ppermute(two_b, "lat", lat_b)
+    (grid,) = call(scatter_kernel, (got,), [(3, 144, 128)], scratch=[(2, 128, 128)], kinds="v")
+    ones_a, ones_b, grid = lax.optimization_barrier((ones_a, ones_b, grid))
+    out, latw, matrix, emitted = call(
+        rows_kernel,
+        (ids, state_one.reshape(N1, 16, 8, 128), meridional_wind, ones_a, ones_b, edge, mixing.reshape(128, 16), grid),
+        [(16, 128, 128), (16, 13, 8, 128), (128, 128), (16, 8, 128)],
         scratch=[
-            (16, 128, 128),
-            (17, 16, 24, 128),
+            (N1, 128, 128),
+            (N1, 16, 24, 128),
             (3, 144, 128),
-            (16, 13, 8, 128),
             (16, 8, 128),
-            (LATMSG, 8, 128),
-            (LATMSG, 8, 128),
+            (MSG1, 8, 128),
+            (MSG1, 8, 128),
             (128, 16),
+            (3, 7, 136, 128),
+            (3, 144, 128),
+            (3, 136, 128),
+            (16, 24, 128),
+            (N1, 128, 128),
         ],
-        kinds="svhhhvh",
-        copies=4,
+        us=5,
+        kinds="shhhhvhv",
+        copies=5,
+        in_hbm=(0,),
     )
     (out,) = call(
-        emit_kernel,
-        (got, mixed, lonw, latw, column),
+        last_kernel,
+        (ids, state_two.reshape(N2, 16, 8, 128), twos_a, twos_b, latw, matrix, emitted, out),
         [(16, 128, 128)],
-        scratch=[(3, 144, 128), (3, 136, 128), (2, 128, 128), (16, 24, 128), (16, 128, 128), (16, 128, 128)],
-        kinds="vhvvv",
-        copies=5,
-        out_spec=pl.BlockSpec(memory_space=pl.ANY),
+        scratch=[
+            (N2, 128, 128),
+            (N2, 16, 24, 128),
+            (N2, 128, 128),
+        ],
+        us=4,
+        kinds="shvvvvvh",
+        copies=3,
+        in_hbm=(0,),
+        aliases={7: 0},
     )
     return out.reshape(shape)
 

time: 61.2 us -> 54.5 us (0.89)
  the two profiles are of different devices: /device:TPU:1 before, /device:TPU:2 now
where the time goes in v3:
time: 54.5 us; the launch traced here: 54.2 us
  starting transfers between devices  24.6 us (45%)
  Pallas kernels  21.6 us (40%)
  waiting for transfers between devices  7.78 us (14%)
    pallas_call x7, Pallas kernels, call(): pl.pallas_call(kernel, out_shape=[pltpu.HBM(s, F32) if n in in_hbm else j...  21.6 us
    all_to_all x1, starting transfers between devices, on_device(): lax.all_to_all(message.reshape(128, 1, ROWS * 128), ('lat', 'lon'), split...  10.2 us
    ppermute x1, starting transfers between devices, on_device(): halo_b = lax.ppermute(pack_b, 'lon', lon_b)  4.68 us
    ppermute x1, starting transfers between devices, on_device(): ones_b = lax.ppermute(one_b, 'lat', lat_b)  4.22 us
    ppermute x1, waiting for transfers between devices, on_device(): ones_b = lax.ppermute(one_b, 'lat', lat_b)  3.28 us
    ppermute x1, waiting for transfers between devices, on_device(): ones_a = lax.ppermute(one_a, 'lat', lat_a)  3.11 us
    ppermute x1, starting transfers between devices, on_device(): twos_b = lax.ppermute(two_b, 'lat', lat_b)  2.89 us
    ppermute x1, starting transfers between devices, on_device(): ones_a = lax.ppermute(one_a, 'lat', lat_a)  1.68 us
  transfers between devices with their start and end apart: 7, of which 3 were waited for; matrix products, arithmetic and copies ran while one was open for 0% of the time, Pallas kernels for 29%

profile of v3, /device:TPU:2, one launch (start us, length us, event | category | flops | bytes accessed | tf_op | source)
XLA Modules:
  0.0 54.2 jit_solution(15848494137067576504)
XLA Ops:
  0.0 0.1 pad_add_fusion.ids
  0.1 2.1 %shard_map.118 = (f32[17,8,128]{2,1,0:T(8,128)S(1)}, f32[17,8,128]{2,1,0:T(8,128)S(1)}, f32[17,128,128]{2,1,0:T(8,128)S(1)}) custom-call(s32[2]{0:T(128)S(1)} %pad_add_fusion.ids, f32[16,128,128]{2,1,0:T(8,128)} %bitcast.17, f32[128,128]{1,0:T(8,128)} %bitcast.20), custom_call_target="tpu_custom_call" | custom-call | bytes 7200000 | tf_op jit(solution)/shard_map/pallas_call | solution.py:526
  2.2 0.1 collective-permute-start
  2.3 4.7 %collective-permute-start.1 = (f32[17,8,128]{2,1,0:T(8,128)S(1)}, f32[17,8,128]{2,1,0:T(8,128)S(1)}, u32[]{:S(2)}, u32[]{:S(2)}) collective-permute-start(f32[17,8,128]{2,1,0:T(8,128)S(1)} %get-tuple-element.28), channel_id=1, source_target_pairs={{0,15},{1,2},{2,1},{3,4},{4,3},{5,6},{6,5},{7,8},{8,7},{9,10},{10,... | collective-permute-start | bytes 208904 | tf_op jit(solution)/shard_map/ppermute | solution.py:565
  7.0 2.9 %shard_map.119 = f32[1280,128]{1,0:T(8,128)} custom-call(bf16[64,512]{1,0:T(8,128)(2,1)} %bitcast.22, s32[1,512]{1,0:T(1,128)} %bitcast.25, s32[1,512]{1,0:T(1,128)} %bitcast.26, bf16[64,256]{1,0:T(8,128)(2,1)} %refs_3_.1, f32[1,256]{1,0:T(1,128)} %bitcast.27, bf16[256,256]{1,0:T(8,128)(2,1)} %refs_5_.1, f32[1,256]{1,0:T(1,128)} %bitcast.28, ...), custom_call_target="tpu_custom_call" | custom-call | bytes 10800000 | tf_op jit(solution)/shard_map/pallas_call | solution.py:526
  9.9 0.0 collective-permute-done.halo_a
  9.9 0.0 collective-permute-done.1.halo_b
  9.9 10.2 %all-to-all-start = ((f32[128,1,1280]{2,1,0:T(1,128)}), f32[128,1,1280]{2,1,0:T(1,128)S(1)}, u32[]{:S(2)}, u32[]{:S(2)}) async-start(f32[128,1,1280]{2,1,0:T(1,128)} %bitcast.12), calls=%async_computation | async-start | bytes 1310720 | tf_op jit(solution)/shard_map/all_to_all | solution.py:600
  20.1 2.5 %shard_map.120 = (f32[8,128,128]{2,1,0:T(8,128)}, f32[111,8,128]{2,1,0:T(8,128)S(1)}, f32[111,8,128]{2,1,0:T(8,128)S(1)}, f32[144,128]{1,0:T(8,128)S(1)}, f32[7,136,128]{2,1,0:T(8,128)S(1)}) custom-call(s32[2]{0:T(128)S(1)} %pad_add_fusion.ids, f32[17,128,128]{2,1,0:T(8,128)S(1)} %get-tuple-element.26.turned, f32[128,128]{1,0:T(8,128)} %bitcast.21, ...), custom_call_target="tpu_custom_call" | custom-call | bytes 10800000 | tf_op jit(solution)/shard_map/pallas_call | solution.py:526
  22.6 1.7 %collective-permute-start.4 = (f32[111,8,128]{2,1,0:T(8,128)S(1)}, f32[111,8,128]{2,1,0:T(8,128)}, u32[]{:S(2)}, u32[]{:S(2)}) collective-permute-start(f32[111,8,128]{2,1,0:T(8,128)S(1)} %get-tuple-element.36), channel_id=1, source_target_pairs={{0,16},{16,0},{32,48},{48,32},{64,80},{80,64},{96,112},{112,96},{1... | collective-permute-start | bytes 1363976 | tf_op jit(solution)/shard_map/ppermute | solution.py:598
  24.3 4.2 %collective-permute-start.5 = (f32[111,8,128]{2,1,0:T(8,128)S(1)}, f32[111,8,128]{2,1,0:T(8,128)}, u32[]{:S(2)}, u32[]{:S(2)}) collective-permute-start(f32[111,8,128]{2,1,0:T(8,128)S(1)} %get-tuple-element.37), channel_id=1, source_target_pairs={{16,32},{32,16},{48,64},{64,48},{80,96},{96,80},{17,33},{33,17},{4... | collective-permute-start | bytes 1363976 | tf_op jit(solution)/shard_map/ppermute | solution.py:599
  28.5 3.1 %shard_map.121 = (f32[8,128,128]{2,1,0:T(8,128)}, f32[96,8,128]{2,1,0:T(8,128)}, f32[96,8,128]{2,1,0:T(8,128)S(1)}) custom-call(s32[2]{0:T(128)S(1)} %pad_add_fusion.ids, f32[17,128,128]{2,1,0:T(8,128)S(1)} %get-tuple-element.26.turned, f32[17,8,128]{2,1,0:T(8,128)S(1)} %collective-permute-done.halo_a, f32[17,8,128]{2,1,0:T(8,128)S(1)} %collective-permute-done.1.halo_b, ...), custom_call_target="tpu_custom_call" | custom-call | bytes 10800000 | tf_op jit(solution)/shard_map/pallas_call | solution.py:526
  31.6 0.9 %collective-permute-start.2 = (f32[96,8,128]{2,1,0:T(8,128)}, f32[96,8,128]{2,1,0:T(8,128)S(1)}, u32[]{:S(2)}, u32[]{:S(2)}) collective-permute-start(f32[96,8,128]{2,1,0:T(8,128)} %get-tuple-element.33), channel_id=1, source_target_pairs={{0,16},{16,0},{32,48},{48,32},{64,80},{80,64},{96,112},{112,96},{1... | collective-permute-start | bytes 1179656 | tf_op jit(solution)/shard_map/ppermute | solution.py:613
  32.5 2.9 %collective-permute-start.3 = (f32[96,8,128]{2,1,0:T(8,128)S(1)}, f32[96,8,128]{2,1,0:T(8,128)S(1)}, u32[]{:S(2)}, u32[]{:S(2)}) collective-permute-start(f32[96,8,128]{2,1,0:T(8,128)S(1)} %get-tuple-element.34), channel_id=1, source_target_pairs={{16,32},{32,16},{48,64},{64,48},{80,96},{96,80},{17,33},{33,17},{4... | collective-permute-start | bytes 1179656 | tf_op jit(solution)/shard_map/ppermute | solution.py:614
  35.4 0.0 all-to-all-done
  35.4 1.5 %shard_map.122.grid_in = f32[3,144,128]{2,1,0:T(8,128)S(1)} custom-call(f32[1280,128]{1,0:T(8,128)S(1)} %bitcast.16), custom_call_target="tpu_custom_call" | custom-call | bytes 7200000 | tf_op jit(solution)/shard_map/pallas_call | solution.py:526
  36.9 3.1 %collective-permute-done.4.a_hbm = f32[111,8,128]{2,1,0:T(8,128)} collective-permute-done((f32[111,8,128]{2,1,0:T(8,128)S(1)}, f32[111,8,128]{2,1,0:T(8,128)}, u32[]{:S(2)}, u32[]{:S(2)}) %collective-permute-start.4) | collective-permute-done | bytes 454688 | tf_op jit(solution)/shard_map/ppermute | solution.py:598
  40.0 3.3 %collective-permute-done.5.b_hbm = f32[111,8,128]{2,1,0:T(8,128)} collective-permute-done((f32[111,8,128]{2,1,0:T(8,128)S(1)}, f32[111,8,128]{2,1,0:T(8,128)}, u32[]{:S(2)}, u32[]{:S(2)}) %collective-permute-start.5) | collective-permute-done | bytes 454688 | tf_op jit(solution)/shard_map/ppermute | solution.py:599
  43.3 5.9 %shard_map.123 = (f32[16,128,128]{2,1,0:T(8,128)}, f32[16,13,8,128]{3,2,1,0:T(8,128)S(1)}, f32[128,128]{1,0:T(8,128)S(1)}, f32[16,8,128]{2,1,0:T(8,128)S(1)}) custom-call(s32[2]{0:T(128)S(1)} %pad_add_fusion.ids, f32[8,16,8,128]{3,2,1,0:T(8,128)} %bitcast.19, f32[16,8,128]{2,1,0:T(8,128)} %merid_hbm.3, f32[111,8,128]{2,1,0:T(8,128)} %collective-permute-done.4.a_hbm, ...), custom_call_target="tpu_custom_call" | custom-call | bytes 18000000 | tf_op jit(solution)/shard_map/pallas_call | solution.py:526
  49.3 0.0 collective-permute-done.2.halo_a
  49.3 1.4 %collective-permute-done.3.halo_b = f32[96,8,128]{2,1,0:T(8,128)S(1)} collective-permute-done((f32[96,8,128]{2,1,0:T(8,128)S(1)}, f32[96,8,128]{2,1,0:T(8,128)S(1)}, u32[]{:S(2)}, u32[]{:S(2)}) %collective-permute-start.3) | collective-permute-done | bytes 393248 | tf_op jit(solution)/shard_map/ppermute | solution.py:614
  50.7 3.5 %shard_map.124 = f32[16,128,128]{2,1,0:T(8,128)} custom-call(s32[2]{0:T(128)S(1)} %pad_add_fusion.ids, f32[8,16,8,128]{3,2,1,0:T(8,128)} %bitcast.18, f32[96,8,128]{2,1,0:T(8,128)S(1)} %collective-permute-done.2.halo_a, f32[96,8,128]{2,1,0:T(8,128)S(1)} %collective-permute-done.3.halo_b, ...), custom_call_target="tpu_custom_call", output_to_operand_aliasing={{}: (7, {})} | custom-call | bytes 14400000 | tf_op jit(solution)/shard_map/pallas_call | solution.py:526
Async XLA Ops:
  2.2 7.7 %collective-permute-start = (f32[17,8,128]{2,1,0:T(8,128)S(1)}, f32[17,8,128]{2,1,0:T(8,128)S(1)}, u32[]{:S(2)}, u32[]{:S(2)}) collective-permute-start(f32[17,8,128]{2,1,0:T(8,128)S(1)} %get-tuple-element.27), channel_id=1, source_target_pairs={{0,1},{1,0},{2,3},{3,2},{4,5},{5,4},{6,7},{7,6},{8,9},{9,8},{10,11... | collective-permute-start | bytes 208904 | tf_op jit(solution)/shard_map/ppermute | solution.py:566
  2.3 7.6 %collective-permute-start.1 = (f32[17,8,128]{2,1,0:T(8,128)S(1)}, f32[17,8,128]{2,1,0:T(8,128)S(1)}, u32[]{:S(2)}, u32[]{:S(2)}) collective-permute-start(f32[17,8,128]{2,1,0:T(8,128)S(1)} %get-tuple-element.28), channel_id=1, source_target_pairs={{0,15},{1,2},{2,1},{3,4},{4,3},{5,6},{6,5},{7,8},{8,7},{9,10},{10,... | collective-permute-start | bytes 208904 | tf_op jit(solution)/shard_map/ppermute | solution.py:565
  9.9 25.5 %all-to-all-start = ((f32[128,1,1280]{2,1,0:T(1,128)}), f32[128,1,1280]{2,1,0:T(1,128)S(1)}, u32[]{:S(2)}, u32[]{:S(2)}) async-start(f32[128,1,1280]{2,1,0:T(1,128)} %bitcast.12), calls=%async_computation | async-start | bytes 1310720 | tf_op jit(solution)/shard_map/all_to_all | solution.py:600
  22.6 17.4 %collective-permute-start.4 = (f32[111,8,128]{2,1,0:T(8,128)S(1)}, f32[111,8,128]{2,1,0:T(8,128)}, u32[]{:S(2)}, u32[]{:S(2)}) collective-permute-start(f32[111,8,128]{2,1,0:T(8,128)S(1)} %get-tuple-element.36), channel_id=1, source_target_pairs={{0,16},{16,0},{32,48},{48,32},{64,80},{80,64},{96,112},{112,96},{1... | collective-permute-start | bytes 1363976 | tf_op jit(solution)/shard_map/ppermute | solution.py:598
  24.3 19.0 %collective-permute-start.5 = (f32[111,8,128]{2,1,0:T(8,128)S(1)}, f32[111,8,128]{2,1,0:T(8,128)}, u32[]{:S(2)}, u32[]{:S(2)}) collective-permute-start(f32[111,8,128]{2,1,0:T(8,128)S(1)} %get-tuple-element.37), channel_id=1, source_target_pairs={{16,32},{32,16},{48,64},{64,48},{80,96},{96,80},{17,33},{33,17},{4... | collective-permute-start | bytes 1363976 | tf_op jit(solution)/shard_map/ppermute | solution.py:599
  31.6 17.7 %collective-permute-start.2 = (f32[96,8,128]{2,1,0:T(8,128)}, f32[96,8,128]{2,1,0:T(8,128)S(1)}, u32[]{:S(2)}, u32[]{:S(2)}) collective-permute-start(f32[96,8,128]{2,1,0:T(8,128)} %get-tuple-element.33), channel_id=1, source_target_pairs={{0,16},{16,0},{32,48},{48,32},{64,80},{80,64},{96,112},{112,96},{1... | collective-permute-start | bytes 1179656 | tf_op jit(solution)/shard_map/ppermute | solution.py:613
  32.5 18.2 %collective-permute-start.3 = (f32[96,8,128]{2,1,0:T(8,128)S(1)}, f32[96,8,128]{2,1,0:T(8,128)S(1)}, u32[]{:S(2)}, u32[]{:S(2)}) collective-permute-start(f32[96,8,128]{2,1,0:T(8,128)S(1)} %get-tuple-element.34), channel_id=1, source_target_pairs={{16,32},{32,16},{48,64},{64,48},{80,96},{96,80},{17,33},{33,17},{4... | collective-permute-start | bytes 1179656 | tf_op jit(solution)/shard_map/ppermute | solution.py:614

commit v4 on v3

--- a/solution.py
+++ b/solution.py
@@ -143,11 +143,12 @@
     return double_weights(w, wl, wh, 0, sub)
 
 
-def pack_kernel(ids, tracers_hbm, zonal_hbm, out_a, out_b, turned, tracers, zonal, sems):
+def pack_kernel(ids, tracers_hbm, zonal_hbm, *refs):
+    flux_in, (out_a, out_b, turned), flux_out, (tracers, zonal, sems) = refs[:8], refs[8:11], refs[11:19], refs[19:]
     odd = (ids[1] & 1) == 1
     chunks = [(zonal_hbm, zonal)]
     chunks += [(tracers_hbm.at[pl.ds(4 * n, 4)], tracers.at[pl.ds(4 * n, 4)]) for n in range(4)]
-    copies = load(chunks, sems)
+    copies = load(chunks + list(zip(flux_in, flux_out)), sems)
 
     def put(t, x):
         x = x.T
@@ -162,14 +163,11 @@
         copies[n + 1].wait()
         for t in range(4 * n, 4 * n + 4):
             put(t, tracers[t])
-
-
-def flux_kernel(*refs):
-    out, sems = refs[8], refs[17]
-    feat, tile, spot, w_in, b_in, w_mid, b_mid, w_out = refs[9:17]
-    for c in load(list(zip(refs[:8], refs[9:17])), sems):
+    for c in copies[5:]:
         c.wait()
 
+
+def flux_kernel(feat, tile, spot, w_in, b_in, w_mid, b_mid, w_out, out):
     def silu(v):
         return (v / (1.0 + jnp.exp(-v))).astype(BF16)
 
@@ -362,10 +360,12 @@
     edge,
     mixing_hbm,
     grid_in,
+    two_hbm,
     out_hbm,
     latw,
     matrix,
     emitted,
+    two,
     swept,
     wide,
     wind,
@@ -383,6 +383,8 @@
     copies = load(
         [(a_hbm, halo_a), (b_hbm, halo_b), (merid_hbm, merid), (mixing_hbm, mixing), (state_hbm, wide.at[:, :, pl.ds(8, 8), :])], sems
     )
+    fetch = pltpu.make_async_copy(two_hbm, two, sems.at[5])
+    fetch.start()
     sub = iota((8, 128), 0)
     keep = jnp.logical_or(sub < 7, ids[0] < 7)
     hi = lax.Precision.HIGHEST
@@ -436,13 +438,15 @@
         out[t] = mix(split, swept[t])
     store = pltpu.make_async_copy(out, out_hbm.at[pl.ds(0, N1)], sems.at[0])
     store.start()
+    fetch.wait()
     store.wait()
 
 
-def last_kernel(ids, state_hbm, halo_a, halo_b, latw, matrix, emitted, _, out_hbm, swept, wide, out, sems):
-    copies = load([(state_hbm, wide.at[:, :, pl.ds(8, 8), :])], sems)
+def last_kernel(ids, state, halo_a, halo_b, latw, matrix, emitted, _, out_hbm, swept, wide, out, sems):
     split = parts(matrix[...])
-    copies[0].wait()
+    for t in range(N2):
+        for k in range(16):
+            wide[t, k, 8:16] = state[t, 8 * k : 8 * k + 8]
     _, four = row_reader(ids, halo_a, halo_b)
     sweep_rows(N2, four, latw, wide, swept)
     half = N2 // 2
@@ -525,7 +529,7 @@
         rooms.append(pltpu.SemaphoreType.DMA((copies,)))
     return pl.pallas_call(
         kernel,
-        out_shape=[pltpu.HBM(s, F32) if n in in_hbm else jax.ShapeDtypeStruct(s, F32) for n, s in enumerate(outs)],
+        out_shape=[pltpu.HBM(s, F32) if n in in_hbm else struct(s) for n, s in enumerate(outs)],
         in_specs=[pl.BlockSpec(memory_space=spec[x]) for x in kinds],
         out_specs=[pl.BlockSpec(memory_space=pltpu.HBM if n in in_hbm else VM) for n in range(len(outs))],
         scratch_shapes=rooms,
@@ -535,6 +539,10 @@
     )(*[pltpu.with_memory_space_constraint(x, pltpu.HBM) if k == "h" else x for x, k in zip(ins, kinds)])
 
 
+def struct(s):
+    return jax.ShapeDtypeStruct(s, F32) if isinstance(s, tuple) else jax.ShapeDtypeStruct(s.shape, s.dtype)
+
+
 def load(pairs, sems):
     copies = [pltpu.make_async_copy(x, y, sems.at[n]) for n, (x, y) in enumerate(pairs)]
     for c in copies:
@@ -549,21 +557,6 @@
     shape = tracers.shape
     tracers = tracers.reshape(16, 128, 128)
     zonal = zonal_wind.reshape(128, 128)
-    pack_a, pack_b, turned = call(
-        pack_kernel,
-        (ids, tracers, zonal),
-        [(17, 8, 128), (17, 8, 128), (17, 128, 128)],
-        scratch=[(16, 128, 128), (128, 128)],
-        us=2,
-        kinds="shh",
-        copies=5,
-    )
-    lon_a = [(i, i ^ 1) for i in range(16)]
-    lon_b = [(i, (i + 1) % 16 if i & 1 else (i - 1) % 16) for i in range(16)]
-    lat_a = [(i, i ^ 1) for i in range(8)]
-    lat_b = [(i, i + 1 if i & 1 else i - 1) for i in range(1, 7)]
-    halo_b = lax.ppermute(pack_b, "lon", lon_b)
-    halo_a = lax.ppermute(pack_a, "lon", lon_a)
     cells = features.shape[0]
     inputs = (
         features.T,
@@ -575,15 +568,22 @@
         b_mid.reshape(1, -1),
         w_out.T,
     )
-    (message,) = call(
-        flux_kernel,
-        inputs,
-        [(128 * ROWS, 128)],
-        scratch=[VM(x.shape, x.dtype) for x in inputs],
-        us=3,
-        kinds="h" * 8,
-        copies=8,
-    )
+    pack_a, pack_b, turned, *inputs = call(
+        pack_kernel,
+        (ids, tracers, zonal) + inputs,
+        [(17, 8, 128), (17, 8, 128), (17, 128, 128)] + list(inputs),
+        scratch=[(16, 128, 128), (128, 128)],
+        us=2,
+        kinds="shh" + "h" * 8,
+        copies=13,
+    )
+    lon_a = [(i, i ^ 1) for i in range(16)]
+    lon_b = [(i, (i + 1) % 16 if i & 1 else (i - 1) % 16) for i in range(16)]
+    lat_a = [(i, i ^ 1) for i in range(8)]
+    lat_b = [(i, i + 1 if i & 1 else i - 1) for i in range(1, 7)]
+    halo_b = lax.ppermute(pack_b, "lon", lon_b)
+    halo_a = lax.ppermute(pack_a, "lon", lon_a)
+    (message,) = call(flux_kernel, inputs, [(128 * ROWS, 128)], us=3, kinds="v" * 8)
     halo_a, halo_b, message = lax.optimization_barrier((halo_a, halo_b, message))
     state_one, one_a, one_b, edge, weights = call(
         lon_first_kernel,
@@ -614,10 +614,10 @@
     twos_b = lax.ppermute(two_b, "lat", lat_b)
     (grid,) = call(scatter_kernel, (got,), [(3, 144, 128)], scratch=[(2, 128, 128)], kinds="v")
     ones_a, ones_b, grid = lax.optimization_barrier((ones_a, ones_b, grid))
-    out, latw, matrix, emitted = call(
+    out, latw, matrix, emitted, state_two = call(
         rows_kernel,
-        (ids, state_one.reshape(N1, 16, 8, 128), meridional_wind, ones_a, ones_b, edge, mixing.reshape(128, 16), grid),
-        [(16, 128, 128), (16, 13, 8, 128), (128, 128), (16, 8, 128)],
+        (ids, state_one.reshape(N1, 16, 8, 128), meridional_wind, ones_a, ones_b, edge, mixing.reshape(128, 16), grid, state_two),
+        [(16, 128, 128), (16, 13, 8, 128), (128, 128), (16, 8, 128), (N2, 128, 128)],
         scratch=[
             (N1, 128, 128),
             (N1, 16, 24, 128),
@@ -633,13 +633,13 @@
             (N1, 128, 128),
         ],
         us=5,
-        kinds="shhhhvhv",
-        copies=5,
+        kinds="shhhhvhvh",
+        copies=6,
         in_hbm=(0,),
     )
     (out,) = call(
         last_kernel,
-        (ids, state_two.reshape(N2, 16, 8, 128), twos_a, twos_b, latw, matrix, emitted, out),
+        (ids, state_two, twos_a, twos_b, latw, matrix, emitted, out),
         [(16, 128, 128)],
         scratch=[
             (N2, 128, 128),
@@ -647,7 +647,7 @@
             (N2, 128, 128),
         ],
         us=4,
-        kinds="shvvvvvh",
+        kinds="svvvvvvh",
         copies=3,
         in_hbm=(0,),
         aliases={7: 0},

time: 54.5 us -> 53.5 us (0.982)
  Pallas kernels: 21.6 us -> 19.6 us
  waiting for transfers between devices: 7.78 us -> 8.67 us
    pallas_call x7, Pallas kernels: 21.6 us -> 19.6 us  [call(): pl.pallas_call(kernel, out_shape=[pltpu.HBM(s, F32) if n in in_hbm else s...]
    ppermute x1, waiting for transfers between devices: 0.01 us -> 0.9 us  [on_device(): halo_b = lax.ppermute(pack_b, 'lon', lon_b)]
  transfers between devices with their start and end apart: 7 -> 7, of which waited for: 3 -> 4; matrix products, arithmetic and copies ran while one was open for 0% -> 0% of each run, Pallas kernels for 29% -> 28%
where the time goes in v4:
time: 53.5 us; the launch traced here: 53.3 us
  starting transfers between devices  24.8 us (46%)
  Pallas kernels  19.6 us (37%)
  waiting for transfers between devices  8.67 us (16%)
    pallas_call x7, Pallas kernels, call(): pl.pallas_call(kernel, out_shape=[pltpu.HBM(s, F32) if n in in_hbm else s...  19.6 us
    all_to_all x1, starting transfers between devices, on_device(): lax.all_to_all(message.reshape(128, 1, ROWS * 128), ('lat', 'lon'), split...  10.4 us
    ppermute x1, starting transfers between devices, on_device(): halo_b = lax.ppermute(pack_b, 'lon', lon_b)  4.68 us
    ppermute x1, starting transfers between devices, on_device(): ones_b = lax.ppermute(one_b, 'lat', lat_b)  4.22 us
    ppermute x1, waiting for transfers between devices, on_device(): ones_b = lax.ppermute(one_b, 'lat', lat_b)  3.28 us
    ppermute x1, waiting for transfers between devices, on_device(): ones_a = lax.ppermute(one_a, 'lat', lat_a)  3.11 us
    ppermute x1, starting transfers between devices, on_device(): twos_b = lax.ppermute(two_b, 'lat', lat_b)  2.89 us
    ppermute x1, starting transfers between devices, on_device(): ones_a = lax.ppermute(one_a, 'lat', lat_a)  1.68 us
  transfers between devices with their start and end apart: 7, of which 4 were waited for; matrix products, arithmetic and copies ran while one was open for 0% of the time, Pallas kernels for 28%

profile of v4, /device:TPU:2, one launch (start us, length us, event | category | flops | bytes accessed | tf_op | source)
XLA Modules:
  0.0 53.3 jit_solution(10055157557910008361)
XLA Ops:
  0.0 0.1 pad_add_fusion.ids
  0.1 2.2 %shard_map.118 = (f32[17,8,128]{2,1,0:T(8,128)S(1)}, f32[17,8,128]{2,1,0:T(8,128)S(1)}, f32[17,128,128]{2,1,0:T(8,128)S(1)}, bf16[64,512]{1,0:T(8,128)(2,1)S(1)}...) custom-call(s32[2]{0:T(128)S(1)} %pad_add_fusion.ids, ...), custom_call_target="tpu_custom_call" | custom-call | bytes 7200000 | tf_op jit(solution)/shard_map/pallas_call | solution.py:530
  2.3 0.1 collective-permute-start
  2.4 4.7 %collective-permute-start.1 = (f32[17,8,128]{2,1,0:T(8,128)S(1)}, f32[17,8,128]{2,1,0:T(8,128)S(1)}, u32[]{:S(2)}, u32[]{:S(2)}) collective-permute-start(f32[17,8,128]{2,1,0:T(8,128)S(1)} %get-tuple-element.37), channel_id=1, source_target_pairs={{0,15},{1,2},{2,1},{3,4},{4,3},{5,6},{6,5},{7,8},{8,7},{9,10},{10,... | collective-permute-start | bytes 208904 | tf_op jit(solution)/shard_map/ppermute | solution.py:584
  7.1 1.8 %shard_map.119 = f32[1280,128]{1,0:T(8,128)} custom-call(bf16[64,512]{1,0:T(8,128)(2,1)S(1)} %get-tuple-element.38.feat, s32[1,512]{1,0:T(1,128)S(1)} %get-tuple-element.39.tile, s32[1,512]{1,0:T(1,128)S(1)} %get-tuple-element.40.spot, bf16[64,256]{1,0:T(8,128)(2,1)S(1)} %get-tuple-element.41.w_in, f32[1,256]{1,0:T(1,128)S(1)} %get-tuple-element.42.b_in, ...), custom_call_target="tpu_custom_call" | custom-call | bytes 10800000 | tf_op jit(solution)/shard_map/pallas_call | solution.py:530
  8.9 0.0 collective-permute-done.halo_a
  8.9 0.9 %collective-permute-done.1.halo_b = f32[17,8,128]{2,1,0:T(8,128)S(1)} collective-permute-done((f32[17,8,128]{2,1,0:T(8,128)S(1)}, f32[17,8,128]{2,1,0:T(8,128)S(1)}, u32[]{:S(2)}, u32[]{:S(2)}) %collective-permute-start.1) | collective-permute-done | bytes 69664 | tf_op jit(solution)/shard_map/ppermute | solution.py:584
  9.8 10.4 %all-to-all-start = ((f32[128,1,1280]{2,1,0:T(1,128)}), f32[128,1,1280]{2,1,0:T(1,128)S(1)}, u32[]{:S(2)}, u32[]{:S(2)}) async-start(f32[128,1,1280]{2,1,0:T(1,128)} %bitcast.11), calls=%async_computation | async-start | bytes 1310720 | tf_op jit(solution)/shard_map/all_to_all | solution.py:600
  20.2 2.5 %shard_map.120 = (f32[8,128,128]{2,1,0:T(8,128)}, f32[111,8,128]{2,1,0:T(8,128)S(1)}, f32[111,8,128]{2,1,0:T(8,128)S(1)}, f32[144,128]{1,0:T(8,128)S(1)}, f32[7,136,128]{2,1,0:T(8,128)S(1)}) custom-call(s32[2]{0:T(128)S(1)} %pad_add_fusion.ids, f32[17,128,128]{2,1,0:T(8,128)S(1)} %get-tuple-element.35.turned, f32[128,128]{1,0:T(8,128)} %bitcast.19, ...), custom_call_target="tpu_custom_call" | custom-call | bytes 10800000 | tf_op jit(solution)/shard_map/pallas_call | solution.py:530
  22.7 1.7 %collective-permute-start.2 = (f32[111,8,128]{2,1,0:T(8,128)S(1)}, f32[111,8,128]{2,1,0:T(8,128)}, u32[]{:S(2)}, u32[]{:S(2)}) collective-permute-start(f32[111,8,128]{2,1,0:T(8,128)S(1)} %get-tuple-element.49), channel_id=1, source_target_pairs={{0,16},{16,0},{32,48},{48,32},{64,80},{80,64},{96,112},{112,96},{1... | collective-permute-start | bytes 1363976 | tf_op jit(solution)/shard_map/ppermute | solution.py:598
  24.4 4.2 %collective-permute-start.3 = (f32[111,8,128]{2,1,0:T(8,128)S(1)}, f32[111,8,128]{2,1,0:T(8,128)}, u32[]{:S(2)}, u32[]{:S(2)}) collective-permute-start(f32[111,8,128]{2,1,0:T(8,128)S(1)} %get-tuple-element.50), channel_id=1, source_target_pairs={{16,32},{32,16},{48,64},{64,48},{80,96},{96,80},{17,33},{33,17},{4... | collective-permute-start | bytes 1363976 | tf_op jit(solution)/shard_map/ppermute | solution.py:599
  28.6 3.1 %shard_map.122 = (f32[8,128,128]{2,1,0:T(8,128)}, f32[96,8,128]{2,1,0:T(8,128)}, f32[96,8,128]{2,1,0:T(8,128)S(1)}) custom-call(s32[2]{0:T(128)S(1)} %pad_add_fusion.ids, f32[17,128,128]{2,1,0:T(8,128)S(1)} %get-tuple-element.35.turned, f32[17,8,128]{2,1,0:T(8,128)S(1)} %collective-permute-done.halo_a, f32[17,8,128]{2,1,0:T(8,128)S(1)} %collective-permute-done.1.halo_b, ...), custom_call_target="tpu_custom_call" | custom-call | bytes 10800000 | tf_op jit(solution)/shard_map/pallas_call | solution.py:530
  31.7 0.9 %collective-permute-start.4 = (f32[96,8,128]{2,1,0:T(8,128)}, f32[96,8,128]{2,1,0:T(8,128)S(1)}, u32[]{:S(2)}, u32[]{:S(2)}) collective-permute-start(f32[96,8,128]{2,1,0:T(8,128)} %get-tuple-element.59), channel_id=1, source_target_pairs={{0,16},{16,0},{32,48},{48,32},{64,80},{80,64},{96,112},{112,96},{1... | collective-permute-start | bytes 1179656 | tf_op jit(solution)/shard_map/ppermute | solution.py:613
  32.6 2.9 %collective-permute-start.5 = (f32[96,8,128]{2,1,0:T(8,128)S(1)}, f32[96,8,128]{2,1,0:T(8,128)S(1)}, u32[]{:S(2)}, u32[]{:S(2)}) collective-permute-start(f32[96,8,128]{2,1,0:T(8,128)S(1)} %get-tuple-element.60), channel_id=1, source_target_pairs={{16,32},{32,16},{48,64},{64,48},{80,96},{96,80},{17,33},{33,17},{4... | collective-permute-start | bytes 1179656 | tf_op jit(solution)/shard_map/ppermute | solution.py:614
  35.5 0.0 all-to-all-done
  35.5 1.5 %shard_map.121.grid_in = f32[3,144,128]{2,1,0:T(8,128)S(1)} custom-call(f32[1280,128]{1,0:T(8,128)S(1)} %bitcast.15), custom_call_target="tpu_custom_call" | custom-call | bytes 7200000 | tf_op jit(solution)/shard_map/pallas_call | solution.py:530
  37.0 3.1 %collective-permute-done.2.a_hbm = f32[111,8,128]{2,1,0:T(8,128)} collective-permute-done((f32[111,8,128]{2,1,0:T(8,128)S(1)}, f32[111,8,128]{2,1,0:T(8,128)}, u32[]{:S(2)}, u32[]{:S(2)}) %collective-permute-start.2) | collective-permute-done | bytes 454688 | tf_op jit(solution)/shard_map/ppermute | solution.py:598
  40.1 3.3 %collective-permute-done.3.b_hbm = f32[111,8,128]{2,1,0:T(8,128)} collective-permute-done((f32[111,8,128]{2,1,0:T(8,128)S(1)}, f32[111,8,128]{2,1,0:T(8,128)}, u32[]{:S(2)}, u32[]{:S(2)}) %collective-permute-start.3) | collective-permute-done | bytes 454688 | tf_op jit(solution)/shard_map/ppermute | solution.py:599
  43.4 6.0 %shard_map.123 = (f32[16,128,128]{2,1,0:T(8,128)}, f32[16,13,8,128]{3,2,1,0:T(8,128)S(1)}, f32[128,128]{1,0:T(8,128)S(1)}, f32[16,8,128]{2,1,0:T(8,128)S(1)}, f32[8,128,128]{2,1,0:T(8,128)S(1)}) custom-call(s32[2]{0:T(128)S(1)} %pad_add_fusion.ids, f32[8,16,8,128]{3,2,1,0:T(8,128)} %bitcast.17, f32[16,8,128]{2,1,0:T(8,128)} %merid_hbm.3, ...), custom_call_target="tpu_custom_call" | custom-call | bytes 18000000 | tf_op jit(solution)/shard_map/pallas_call | solution.py:530
  49.4 0.0 collective-permute-done.4.halo_a
  49.4 1.4 %collective-permute-done.5.halo_b = f32[96,8,128]{2,1,0:T(8,128)S(1)} collective-permute-done((f32[96,8,128]{2,1,0:T(8,128)S(1)}, f32[96,8,128]{2,1,0:T(8,128)S(1)}, u32[]{:S(2)}, u32[]{:S(2)}) %collective-permute-start.5) | collective-permute-done | bytes 393248 | tf_op jit(solution)/shard_map/ppermute | solution.py:614
  50.8 2.5 %shard_map.124 = f32[16,128,128]{2,1,0:T(8,128)} custom-call(s32[2]{0:T(128)S(1)} %pad_add_fusion.ids, f32[8,128,128]{2,1,0:T(8,128)S(1)} %get-tuple-element.58.state, f32[96,8,128]{2,1,0:T(8,128)S(1)} %collective-permute-done.4.halo_a, f32[96,8,128]{2,1,0:T(8,128)S(1)} %collective-permute-done.5.halo_b, ...), custom_call_target="tpu_custom_call", output_to_operand_aliasing={{}: (7, {})} | custom-call | bytes 14400000 | tf_op jit(solution)/shard_map/pallas_call | solution.py:530
Async XLA Ops:
  2.3 6.6 %collective-permute-start = (f32[17,8,128]{2,1,0:T(8,128)S(1)}, f32[17,8,128]{2,1,0:T(8,128)S(1)}, u32[]{:S(2)}, u32[]{:S(2)}) collective-permute-start(f32[17,8,128]{2,1,0:T(8,128)S(1)} %get-tuple-element.36), channel_id=1, source_target_pairs={{0,1},{1,0},{2,3},{3,2},{4,5},{5,4},{6,7},{7,6},{8,9},{9,8},{10,11... | collective-permute-start | bytes 208904 | tf_op jit(solution)/shard_map/ppermute | solution.py:585
  2.4 7.4 %collective-permute-start.1 = (f32[17,8,128]{2,1,0:T(8,128)S(1)}, f32[17,8,128]{2,1,0:T(8,128)S(1)}, u32[]{:S(2)}, u32[]{:S(2)}) collective-permute-start(f32[17,8,128]{2,1,0:T(8,128)S(1)} %get-tuple-element.37), channel_id=1, source_target_pairs={{0,15},{1,2},{2,1},{3,4},{4,3},{5,6},{6,5},{7,8},{8,7},{9,10},{10,... | collective-permute-start | bytes 208904 | tf_op jit(solution)/shard_map/ppermute | solution.py:584
  9.8 25.7 %all-to-all-start = ((f32[128,1,1280]{2,1,0:T(1,128)}), f32[128,1,1280]{2,1,0:T(1,128)S(1)}, u32[]{:S(2)}, u32[]{:S(2)}) async-start(f32[128,1,1280]{2,1,0:T(1,128)} %bitcast.11), calls=%async_computation | async-start | bytes 1310720 | tf_op jit(solution)/shard_map/all_to_all | solution.py:600
  22.7 17.4 %collective-permute-start.2 = (f32[111,8,128]{2,1,0:T(8,128)S(1)}, f32[111,8,128]{2,1,0:T(8,128)}, u32[]{:S(2)}, u32[]{:S(2)}) collective-permute-start(f32[111,8,128]{2,1,0:T(8,128)S(1)} %get-tuple-element.49), channel_id=1, source_target_pairs={{0,16},{16,0},{32,48},{48,32},{64,80},{80,64},{96,112},{112,96},{1... | collective-permute-start | bytes 1363976 | tf_op jit(solution)/shard_map/ppermute | solution.py:598
  24.4 19.0 %collective-permute-start.3 = (f32[111,8,128]{2,1,0:T(8,128)S(1)}, f32[111,8,128]{2,1,0:T(8,128)}, u32[]{:S(2)}, u32[]{:S(2)}) collective-permute-start(f32[111,8,128]{2,1,0:T(8,128)S(1)} %get-tuple-element.50), channel_id=1, source_target_pairs={{16,32},{32,16},{48,64},{64,48},{80,96},{96,80},{17,33},{33,17},{4... | collective-permute-start | bytes 1363976 | tf_op jit(solution)/shard_map/ppermute | solution.py:599
  31.7 17.7 %collective-permute-start.4 = (f32[96,8,128]{2,1,0:T(8,128)}, f32[96,8,128]{2,1,0:T(8,128)S(1)}, u32[]{:S(2)}, u32[]{:S(2)}) collective-permute-start(f32[96,8,128]{2,1,0:T(8,128)} %get-tuple-element.59), channel_id=1, source_target_pairs={{0,16},{16,0},{32,48},{48,32},{64,80},{80,64},{96,112},{112,96},{1... | collective-permute-start | bytes 1179656 | tf_op jit(solution)/shard_map/ppermute | solution.py:613
  32.6 18.2 %collective-permute-start.5 = (f32[96,8,128]{2,1,0:T(8,128)S(1)}, f32[96,8,128]{2,1,0:T(8,128)S(1)}, u32[]{:S(2)}, u32[]{:S(2)}) collective-permute-start(f32[96,8,128]{2,1,0:T(8,128)S(1)} %get-tuple-element.60), channel_id=1, source_target_pairs={{16,32},{32,16},{48,64},{64,48},{80,96},{96,80},{17,33},{33,17},{4... | collective-permute-start | bytes 1179656 | tf_op jit(solution)/shard_map/ppermute | solution.py:614

commit v5 on v4

--- a/solution.py
+++ b/solution.py
@@ -10,7 +10,7 @@
 NT = (((1,), (1,)), ((), ()))
 TN = (((0,), (0,)), ((), ()))
 ROWS = 10
-N1 = 8
+N1 = 9
 N2 = 16 - N1
 WIND = 12 * N1
 MSG1 = WIND + 15
@@ -595,8 +595,8 @@
         copies=3,
         in_hbm=(0,),
     )
+    ones_b = lax.ppermute(one_b, "lat", lat_b)
     ones_a = lax.ppermute(one_a, "lat", lat_a)
-    ones_b = lax.ppermute(one_b, "lat", lat_b)
     got = lax.all_to_all(
         message.reshape(128, 1, ROWS * 128), ("lat", "lon"), split_axis=0, concat_axis=0, tiled=True
     ).reshape(128 * ROWS, 128)
@@ -613,7 +613,7 @@
     twos_a = lax.ppermute(two_a, "lat", lat_a)
     twos_b = lax.ppermute(two_b, "lat", lat_b)
     (grid,) = call(scatter_kernel, (got,), [(3, 144, 128)], scratch=[(2, 128, 128)], kinds="v")
-    ones_a, ones_b, grid = lax.optimization_barrier((ones_a, ones_b, grid))
+    ones_b, ones_a, grid = lax.optimization_barrier((ones_b, ones_a, grid))
     out, latw, matrix, emitted, state_two = call(
         rows_kernel,
         (ids, state_one.reshape(N1, 16, 8, 128), meridional_wind, ones_a, ones_b, edge, mixing.reshape(128, 16), grid, state_two),

time: 53.5 us -> 53.4 us (level)
  waiting for transfers between devices: 8.67 us -> 8 us
    ppermute x1, waiting for transfers between devices: 3.28 us -> 6.44 us  [on_device(): ones_b = lax.ppermute(one_b, 'lat', lat_b)]
    ppermute x1, waiting for transfers between devices: 3.11 us -> 0.01 us  [on_device(): ones_a = lax.ppermute(one_a, 'lat', lat_a)]
    ppermute x1, starting transfers between devices: 1.68 us -> 0.09 us  [on_device(): ones_a = lax.ppermute(one_a, 'lat', lat_a)]
    ppermute x1, starting transfers between devices: 0.93 us -> 2.09 us  [on_device(): twos_a = lax.ppermute(two_a, 'lat', lat_a)]
    ppermute x1, starting transfers between devices: 4.22 us -> 5.24 us  [on_device(): ones_b = lax.ppermute(one_b, 'lat', lat_b)]
    ppermute x1, waiting for transfers between devices: 1.37 us -> 0.65 us  [on_device(): twos_b = lax.ppermute(two_b, 'lat', lat_b)]
  transfers between devices with their start and end apart: 7 -> 7, of which waited for: 4 -> 3; matrix products, arithmetic and copies ran while one was open for 0% -> 0% of each run, Pallas kernels for 28% -> 28%
where the time goes in v5:
time: 53.4 us; the launch traced here: 53.2 us
  starting transfers between devices  25.2 us (47%)
  Pallas kernels  19.7 us (37%)
  waiting for transfers between devices  8 us (15%)
    pallas_call x7, Pallas kernels, call(): pl.pallas_call(kernel, out_shape=[pltpu.HBM(s, F32) if n in in_hbm else s...  19.7 us
    all_to_all x1, starting transfers between devices, on_device(): lax.all_to_all(message.reshape(128, 1, ROWS * 128), ('lat', 'lon'), split...  10.4 us
    ppermute x1, waiting for transfers between devices, on_device(): ones_b = lax.ppermute(one_b, 'lat', lat_b)  6.44 us
    ppermute x1, starting transfers between devices, on_device(): ones_b = lax.ppermute(one_b, 'lat', lat_b)  5.24 us
    ppermute x1, starting transfers between devices, on_device(): halo_b = lax.ppermute(pack_b, 'lon', lon_b)  4.68 us
    ppermute x1, starting transfers between devices, on_device(): twos_b = lax.ppermute(two_b, 'lat', lat_b)  2.7 us
    ppermute x1, starting transfers between devices, on_device(): twos_a = lax.ppermute(two_a, 'lat', lat_a)  2.09 us
  transfers between devices with their start and end apart: 7, of which 3 were waited for; matrix products, arithmetic and copies ran while one was open for 0% of the time, Pallas kernels for 28%

profile of v5, /device:TPU:2, one launch (start us, length us, event | category | flops | bytes accessed | tf_op | source)
XLA Modules:
  0.0 53.2 jit_solution(111725265747097600)
XLA Ops:
  0.0 0.1 pad_add_fusion.ids
  0.1 2.2 %shard_map.118 = (f32[17,8,128]{2,1,0:T(8,128)S(1)}, f32[17,8,128]{2,1,0:T(8,128)S(1)}, f32[17,128,128]{2,1,0:T(8,128)S(1)}, bf16[64,512]{1,0:T(8,128)(2,1)S(1)}...) custom-call(s32[2]{0:T(128)S(1)} %pad_add_fusion.ids, ...), custom_call_target="tpu_custom_call" | custom-call | bytes 7200000 | tf_op jit(solution)/shard_map/pallas_call | solution.py:530
  2.3 0.1 collective-permute-start
  2.4 4.7 %collective-permute-start.1 = (f32[17,8,128]{2,1,0:T(8,128)S(1)}, f32[17,8,128]{2,1,0:T(8,128)S(1)}, u32[]{:S(2)}, u32[]{:S(2)}) collective-permute-start(f32[17,8,128]{2,1,0:T(8,128)S(1)} %get-tuple-element.37), channel_id=1, source_target_pairs={{0,15},{1,2},{2,1},{3,4},{4,3},{5,6},{6,5},{7,8},{8,7},{9,10},{10,... | collective-permute-start | bytes 208904 | tf_op jit(solution)/shard_map/ppermute | solution.py:584
  7.1 1.8 %shard_map.119 = f32[1280,128]{1,0:T(8,128)} custom-call(bf16[64,512]{1,0:T(8,128)(2,1)S(1)} %get-tuple-element.38.feat, s32[1,512]{1,0:T(1,128)S(1)} %get-tuple-element.39.tile, s32[1,512]{1,0:T(1,128)S(1)} %get-tuple-element.40.spot, bf16[64,256]{1,0:T(8,128)(2,1)S(1)} %get-tuple-element.41.w_in, f32[1,256]{1,0:T(1,128)S(1)} %get-tuple-element.42.b_in, ...), custom_call_target="tpu_custom_call" | custom-call | bytes 10800000 | tf_op jit(solution)/shard_map/pallas_call | solution.py:530
  8.9 0.0 collective-permute-done.halo_a
  8.9 0.9 %collective-permute-done.1.halo_b = f32[17,8,128]{2,1,0:T(8,128)S(1)} collective-permute-done((f32[17,8,128]{2,1,0:T(8,128)S(1)}, f32[17,8,128]{2,1,0:T(8,128)S(1)}, u32[]{:S(2)}, u32[]{:S(2)}) %collective-permute-start.1) | collective-permute-done | bytes 69664 | tf_op jit(solution)/shard_map/ppermute | solution.py:584
  9.8 10.4 %all-to-all-start = ((f32[128,1,1280]{2,1,0:T(1,128)}), f32[128,1,1280]{2,1,0:T(1,128)S(1)}, u32[]{:S(2)}, u32[]{:S(2)}) async-start(f32[128,1,1280]{2,1,0:T(1,128)} %bitcast.11), calls=%async_computation | async-start | bytes 1310720 | tf_op jit(solution)/shard_map/all_to_all | solution.py:600
  20.2 2.7 %shard_map.120 = (f32[9,128,128]{2,1,0:T(8,128)}, f32[123,8,128]{2,1,0:T(8,128)S(1)}, f32[123,8,128]{2,1,0:T(8,128)S(1)}, f32[144,128]{1,0:T(8,128)S(1)}, f32[7,136,128]{2,1,0:T(8,128)S(1)}) custom-call(s32[2]{0:T(128)S(1)} %pad_add_fusion.ids, f32[17,128,128]{2,1,0:T(8,128)S(1)} %get-tuple-element.35.turned, f32[128,128]{1,0:T(8,128)} %bitcast.19, ...), custom_call_target="tpu_custom_call" | custom-call | bytes 10800000 | tf_op jit(solution)/shard_map/pallas_call | solution.py:530
  22.9 5.2 %collective-permute-start.2 = (f32[123,8,128]{2,1,0:T(8,128)S(1)}, f32[123,8,128]{2,1,0:T(8,128)}, u32[]{:S(2)}, u32[]{:S(2)}) collective-permute-start(f32[123,8,128]{2,1,0:T(8,128)S(1)} %get-tuple-element.49), channel_id=1, source_target_pairs={{16,32},{32,16},{48,64},{64,48},{80,96},{96,80},{17,33},{33,17},{4... | collective-permute-start | bytes 1511432 | tf_op jit(solution)/shard_map/ppermute | solution.py:598
  28.1 0.1 collective-permute-start.3
  28.2 3.0 %shard_map.122 = (f32[7,128,128]{2,1,0:T(8,128)}, f32[84,8,128]{2,1,0:T(8,128)}, f32[84,8,128]{2,1,0:T(8,128)S(1)}) custom-call(s32[2]{0:T(128)S(1)} %pad_add_fusion.ids, f32[17,128,128]{2,1,0:T(8,128)S(1)} %get-tuple-element.35.turned, f32[17,8,128]{2,1,0:T(8,128)S(1)} %collective-permute-done.halo_a, f32[17,8,128]{2,1,0:T(8,128)S(1)} %collective-permute-done.1.halo_b, ...), custom_call_target="tpu_custom_call" | custom-call | bytes 10800000 | tf_op jit(solution)/shard_map/pallas_call | solution.py:530
  31.2 2.1 %collective-permute-start.4 = (f32[84,8,128]{2,1,0:T(8,128)}, f32[84,8,128]{2,1,0:T(8,128)S(1)}, u32[]{:S(2)}, u32[]{:S(2)}) collective-permute-start(f32[84,8,128]{2,1,0:T(8,128)} %get-tuple-element.59), channel_id=1, source_target_pairs={{0,16},{16,0},{32,48},{48,32},{64,80},{80,64},{96,112},{112,96},{1... | collective-permute-start | bytes 1032200 | tf_op jit(solution)/shard_map/ppermute | solution.py:613
  33.3 2.7 %collective-permute-start.5 = (f32[84,8,128]{2,1,0:T(8,128)S(1)}, f32[84,8,128]{2,1,0:T(8,128)S(1)}, u32[]{:S(2)}, u32[]{:S(2)}) collective-permute-start(f32[84,8,128]{2,1,0:T(8,128)S(1)} %get-tuple-element.60), channel_id=1, source_target_pairs={{16,32},{32,16},{48,64},{64,48},{80,96},{96,80},{17,33},{33,17},{4... | collective-permute-start | bytes 1032200 | tf_op jit(solution)/shard_map/ppermute | solution.py:614
  36.0 0.0 all-to-all-done
  36.0 1.5 %shard_map.121.grid_in = f32[3,144,128]{2,1,0:T(8,128)S(1)} custom-call(f32[1280,128]{1,0:T(8,128)S(1)} %bitcast.15), custom_call_target="tpu_custom_call" | custom-call | bytes 7200000 | tf_op jit(solution)/shard_map/pallas_call | solution.py:530
  37.5 6.4 %collective-permute-done.2.b_hbm = f32[123,8,128]{2,1,0:T(8,128)} collective-permute-done((f32[123,8,128]{2,1,0:T(8,128)S(1)}, f32[123,8,128]{2,1,0:T(8,128)}, u32[]{:S(2)}, u32[]{:S(2)}) %collective-permute-start.2) | collective-permute-done | bytes 503840 | tf_op jit(solution)/shard_map/ppermute | solution.py:598
  44.0 0.0 collective-permute-done.3.a_hbm
  44.0 6.1 %shard_map.123 = (f32[16,128,128]{2,1,0:T(8,128)}, f32[16,13,8,128]{3,2,1,0:T(8,128)S(1)}, f32[128,128]{1,0:T(8,128)S(1)}, f32[16,8,128]{2,1,0:T(8,128)S(1)}, f32[7,128,128]{2,1,0:T(8,128)S(1)}) custom-call(s32[2]{0:T(128)S(1)} %pad_add_fusion.ids, f32[9,16,8,128]{3,2,1,0:T(8,128)} %bitcast.17, f32[16,8,128]{2,1,0:T(8,128)} %merid_hbm.3, ...), custom_call_target="tpu_custom_call" | custom-call | bytes 18000000 | tf_op jit(solution)/shard_map/pallas_call | solution.py:530
  50.1 0.0 collective-permute-done.4.halo_a
  50.1 0.7 %collective-permute-done.5.halo_b = f32[84,8,128]{2,1,0:T(8,128)S(1)} collective-permute-done((f32[84,8,128]{2,1,0:T(8,128)S(1)}, f32[84,8,128]{2,1,0:T(8,128)S(1)}, u32[]{:S(2)}, u32[]{:S(2)}) %collective-permute-start.5) | collective-permute-done | bytes 344096 | tf_op jit(solution)/shard_map/ppermute | solution.py:614
  50.8 2.4 %shard_map.124 = f32[16,128,128]{2,1,0:T(8,128)} custom-call(s32[2]{0:T(128)S(1)} %pad_add_fusion.ids, f32[7,128,128]{2,1,0:T(8,128)S(1)} %get-tuple-element.58.state, f32[84,8,128]{2,1,0:T(8,128)S(1)} %collective-permute-done.4.halo_a, f32[84,8,128]{2,1,0:T(8,128)S(1)} %collective-permute-done.5.halo_b, ...), custom_call_target="tpu_custom_call", output_to_operand_aliasing={{}: (7, {})} | custom-call | bytes 14400000 | tf_op jit(solution)/shard_map/pallas_call | solution.py:530
Async XLA Ops:
  2.3 6.6 %collective-permute-start = (f32[17,8,128]{2,1,0:T(8,128)S(1)}, f32[17,8,128]{2,1,0:T(8,128)S(1)}, u32[]{:S(2)}, u32[]{:S(2)}) collective-permute-start(f32[17,8,128]{2,1,0:T(8,128)S(1)} %get-tuple-element.36), channel_id=1, source_target_pairs={{0,1},{1,0},{2,3},{3,2},{4,5},{5,4},{6,7},{7,6},{8,9},{9,8},{10,11... | collective-permute-start | bytes 208904 | tf_op jit(solution)/shard_map/ppermute | solution.py:585
  2.4 7.4 %collective-permute-start.1 = (f32[17,8,128]{2,1,0:T(8,128)S(1)}, f32[17,8,128]{2,1,0:T(8,128)S(1)}, u32[]{:S(2)}, u32[]{:S(2)}) collective-permute-start(f32[17,8,128]{2,1,0:T(8,128)S(1)} %get-tuple-element.37), channel_id=1, source_target_pairs={{0,15},{1,2},{2,1},{3,4},{4,3},{5,6},{6,5},{7,8},{8,7},{9,10},{10,... | collective-permute-start | bytes 208904 | tf_op jit(solution)/shard_map/ppermute | solution.py:584
  9.8 26.2 %all-to-all-start = ((f32[128,1,1280]{2,1,0:T(1,128)}), f32[128,1,1280]{2,1,0:T(1,128)S(1)}, u32[]{:S(2)}, u32[]{:S(2)}) async-start(f32[128,1,1280]{2,1,0:T(1,128)} %bitcast.11), calls=%async_computation | async-start | bytes 1310720 | tf_op jit(solution)/shard_map/all_to_all | solution.py:600
  22.9 21.1 %collective-permute-start.2 = (f32[123,8,128]{2,1,0:T(8,128)S(1)}, f32[123,8,128]{2,1,0:T(8,128)}, u32[]{:S(2)}, u32[]{:S(2)}) collective-permute-start(f32[123,8,128]{2,1,0:T(8,128)S(1)} %get-tuple-element.49), channel_id=1, source_target_pairs={{16,32},{32,16},{48,64},{64,48},{80,96},{96,80},{17,33},{33,17},{4... | collective-permute-start | bytes 1511432 | tf_op jit(solution)/shard_map/ppermute | solution.py:598
  28.1 15.9 %collective-permute-start.3 = (f32[123,8,128]{2,1,0:T(8,128)S(1)}, f32[123,8,128]{2,1,0:T(8,128)}, u32[]{:S(2)}, u32[]{:S(2)}) collective-permute-start(f32[123,8,128]{2,1,0:T(8,128)S(1)} %get-tuple-element.50), channel_id=1, source_target_pairs={{0,16},{16,0},{32,48},{48,32},{64,80},{80,64},{96,112},{112,96},{1... | collective-permute-start | bytes 1511432 | tf_op jit(solution)/shard_map/ppermute | solution.py:599
  31.2 18.9 %collective-permute-start.4 = (f32[84,8,128]{2,1,0:T(8,128)}, f32[84,8,128]{2,1,0:T(8,128)S(1)}, u32[]{:S(2)}, u32[]{:S(2)}) collective-permute-start(f32[84,8,128]{2,1,0:T(8,128)} %get-tuple-element.59), channel_id=1, source_target_pairs={{0,16},{16,0},{32,48},{48,32},{64,80},{80,64},{96,112},{112,96},{1... | collective-permute-start | bytes 1032200 | tf_op jit(solution)/shard_map/ppermute | solution.py:613
  33.3 17.5 %collective-permute-start.5 = (f32[84,8,128]{2,1,0:T(8,128)S(1)}, f32[84,8,128]{2,1,0:T(8,128)S(1)}, u32[]{:S(2)}, u32[]{:S(2)}) collective-permute-start(f32[84,8,128]{2,1,0:T(8,128)S(1)} %get-tuple-element.60), channel_id=1, source_target_pairs={{16,32},{32,16},{48,64},{64,48},{80,96},{96,80},{17,33},{33,17},{4... | collective-permute-start | bytes 1032200 | tf_op jit(solution)/shard_map/ppermute | solution.py:614
